TPU v7x, 256 devices: a whole 4x4x8 slice. The times are simulated.
256 devices in a mesh: tm: 16 (over y, z_hi), gx: 4 (over x), gy: 4 (over z_lo, core).
Axes of the slice: x: 4, y: 4, z: 8 (z_hi: 4, z_lo: 2; z = z_hi * 2 + z_lo), core: 2. Of those that a mesh axis runs over, the one named last changes fastest.
Arguments:
- state: float32 [16, 3, 64, 64, 128], P('tm', None, 'gx', 'gy'), may hold values from -6 to 6
- waveform: float32 [16, 4], P('tm'), may hold values from -9 to 9
- conductivity: float32 [16], replicated, may hold values from 0.1 to 1
- layer_map: int32 [64, 64, 128], P('gx', 'gy'), may hold values from 0 to 15
- loop_mask: int32 [64, 64, 128], P('gx', 'gy'), may hold values 0 or 1
Outputs:
- next_state: float32 [16, 3, 64, 64, 128], P('tm', None, 'gx', 'gy')
All inputs are finite; a program needn't handle non-finite values. No bound on the sum of `loop_mask` on one device may be relied on, other than what follows from the above.
Results may differ from a plain program's by a relative error of at most 0.0001.
Values sent between devices are 32-bit elements; how exact they have to be, the bound alone decides.
A program may use at most 128 MiB of HBM per device.

v0:
```python
import jax
import jax.numpy as jnp
from jax import lax
from jax.sharding import PartitionSpec as P

DT = 0.015


def padded(value, sides, width):
    for axis, dim in sides:
        size, length = (lax.axis_size(axis), value.shape[dim])
        up = [(i, (i + 1) % size) for i in range(size - 1)]
        down = [(j, i) for i, j in up]
        last = lax.slice_in_dim(value, length - width, length, axis=dim)
        first = lax.slice_in_dim(value, 0, width, axis=dim)
        before = lax.ppermute(last, axis, up)
        after = lax.ppermute(first, axis, down)
        value = jnp.concatenate([before, value, after], axis=dim)
    return value


def passed_along(value, axis, steps):
    count = lax.axis_size(axis)
    first, last = (max(0, -steps), min(count, count - steps))
    return lax.ppermute(value, axis, [(source, source + steps) for source in range(first, last)])


def diff_ahead(values, axis):
    size = values.shape[axis]
    later = lax.slice_in_dim(values, 1, size, axis=axis)
    edge = jnp.zeros_like(lax.slice_in_dim(values, 0, 1, axis=axis))
    return jnp.concatenate([later, edge], axis=axis) - values


def diff_behind(values, axis):
    size = values.shape[axis]
    earlier = lax.slice_in_dim(values, 0, size - 1, axis=axis)
    edge = jnp.zeros_like(lax.slice_in_dim(values, 0, 1, axis=axis))
    return values - jnp.concatenate([edge, earlier], axis=axis)


def curl_curl(field):
    field_zero, field_one, field_two = (field[0], field[1], field[2])
    twist_zero = diff_ahead(field_two, 1) - diff_ahead(field_one, 2)
    twist_one = diff_ahead(field_zero, 2) - diff_ahead(field_two, 0)
    twist_two = diff_ahead(field_one, 0) - diff_ahead(field_zero, 1)
    back_zero = diff_behind(twist_two, 1) - diff_behind(twist_one, 2)
    back_one = diff_behind(twist_zero, 2) - diff_behind(twist_two, 0)
    back_two = diff_behind(twist_one, 0) - diff_behind(twist_zero, 1)
    return jnp.stack([back_zero, back_one, back_two])


def fine_step(field, kappa, drive, pulse):
    moved = field - DT * kappa * curl_curl(field)
    return jnp.stack([moved[0] - DT * pulse * drive, moved[1], moved[2]])


def coarse_step(coarse, coarse_kappa):
    return coarse - 4.0 * DT * coarse_kappa * (curl_curl(coarse) * 0.25)


def restrict(field):
    comps, size_a, size_b, size_c = field.shape
    blocks = field.reshape(comps, size_a // 2, 2, size_b // 2, 2, size_c // 2, 2)
    return jnp.mean(blocks, axis=(2, 4, 6))


def prolong(coarse):
    return jnp.repeat(jnp.repeat(jnp.repeat(coarse, 2, axis=1), 2, axis=2), 2, axis=3)


def body(state, waveform, conductivity, layer_map, loop_mask):
    field_start = state[0]
    pulses = waveform[0]
    steps_count = pulses.shape[0]
    inverse = 1.0 / conductivity
    kappa = jnp.zeros(layer_map.shape, jnp.float32)
    for layer in range(conductivity.shape[0]):
        kappa = kappa + jnp.where(layer_map == layer, inverse[layer], 0.0)
    drive = kappa * loop_mask.astype(jnp.float32)
    coarse_kappa = restrict(kappa[None])[0]
    padded_coarse_kappa = jnp.pad(coarse_kappa, ((1, 1), (1, 1), (0, 0)))
    padded_kappa = jnp.pad(kappa, ((1, 1), (1, 1), (0, 0)))
    padded_drive = jnp.pad(drive, ((1, 1), (1, 1), (0, 0)))
    field = field_start
    for turn in range(steps_count):
        widened = padded(field, (("gx", 1), ("gy", 2)), 1)
        field = fine_step(widened, padded_kappa, padded_drive, pulses[turn])[:, 1:-1, 1:-1]

    def coarse_map(coarse):
        widened = padded(coarse, (("gx", 1), ("gy", 2)), 1)
        return coarse_step(widened, padded_coarse_kappa)[:, 1:-1, 1:-1]

    start = restrict(field_start)
    offset = restrict(field) - coarse_map(start)
    position = lax.axis_index("tm")
    slice_count = lax.axis_size("tm")

    def turn_handed(turn, coarse):
        advanced = coarse_map(coarse) + offset
        received = passed_along(advanced, "tm", 1)
        return jnp.where(position == 0, start, received)

    coarse = lax.fori_loop(0, slice_count - 1, turn_handed, start)
    result = field + prolong(coarse_map(coarse - start))
    return result[None]


def solution(mesh):
    placed = (
        P("tm", None, "gx", "gy", None),
        P("tm", None),
        P(),
        P("gx", "gy", None),
        P("gx", "gy", None),
    )
    return jax.shard_map(
        body, mesh=mesh, in_specs=placed, out_specs=P("tm", None, "gx", "gy", None), check_vma=False
    )
```

profile of v0, /device:TPU:24, one launch (start us, length us, event | category | flops | bytes accessed | tf_op | source)
XLA Modules:
  0.0 579.1 jit_solution(13860018178754330281)
XLA Ops:
  0.0 27.3 %reshape_squeeze.3 = f32[3,8,2,8,2,64,2]{6,5,4,3,2,1,0:T(8,128)} reshape(f32[1,3,16,16,128]{4,3,2,1,0:T(8,128)} %param.7) | data formatting | bytes 786432 | tf_op jit(solution)/shard_map/reshape;squeeze | solution.py:64
  27.3 9.5 %reduce_sum.27 = f32[3,8,8,64]{3,2,1,0:T(8,128)S(1)} reduce(f32[3,8,2,8,2,64,2]{6,5,4,3,2,1,0:T(8,128)} %reshape_squeeze.3, f32[]{:T(128)} %constant.85.clone.1), dimensions={2,4,6}, to_apply=%region_0.1 | reduce | flops 86016 | bytes 442372 | tf_op jit(solution)/shard_map/reduce_sum | solution.py:65
  41.6 4.5 collective-permute-start.5
  48.2 10.3 %convert_multiply_fusion = (f32[16,16,128]{2,1,0:T(8,128)S(1)}, f32[16,16,128]{2,1,0:T(8,128)S(1)}) fusion(s32[16,16,128]{2,1,0:T(8,128)S(1)} %copy-done.4, f32[]{:T(128)} %bitcast.24, s32[16,16,128]{2,1,0:T(8,128)S(1)} %copy-done.5, f32[]{:T(128)} %bitcast.23, f32[]{:T(128)} %bitcast.22, f32[]{:T(128)} %bitcast.21, f32[]{:T(128)} %bitcast.20, f32[]{:T(128)} %bitcast.19, ...), kind=kLoop, calls=%fused_computation.108 | loop fusion | flops 1605632 | bytes 524352 | tf_op jit(solution)/shard_map/mul | solution.py:80
  58.5 9.8 %reshape_broadcast_in_dim.3 = f32[8,2,8,2,64,2]{5,4,3,2,1,0:T(8,128)} reshape(f32[16,16,128]{2,1,0:T(8,128)S(1)} %get-tuple-element.136) | data formatting | bytes 262144 | tf_op jit(solution)/shard_map/reshape;broadcast_in_dim | solution.py:64
  79.1 4.5 collective-permute-start.7
  90.5 5.2 collective-permute-start.9
  111.3 4.2 collective-permute-done.14
  129.3 4.2 collective-permute-done.18
  142.0 26.6 %reshape.63 = f32[3,8,2,8,2,64,2]{6,5,4,3,2,1,0:T(8,128)} reshape(f32[3,16,16,128]{3,2,1,0:T(8,128)S(1)} %pad_maximum_fusion.7) | data formatting | bytes 786432 | tf_op jit(solution)/shard_map/reshape | solution.py:64
  168.5 9.4 %reduce_sum.29 = f32[3,8,8,64]{3,2,1,0:T(8,128)S(1)} reduce(f32[3,8,2,8,2,64,2]{6,5,4,3,2,1,0:T(8,128)} %reshape.63, f32[]{:T(128)} %constant.85.clone.1), dimensions={2,4,6}, to_apply=%region_2.3 | reduce | flops 86016 | bytes 442372 | tf_op jit(solution)/shard_map/reduce_sum | solution.py:65
  178.0 371.6 %while.14 = (s32[]{:T(128)}, f32[3,8,8,64]{3,2,1,0:T(8,128)S(1)}, pred[]{:T(512)}, f32[10,10,64]{2,1,0:T(8,128)S(1)}, f32[3,8,8,64]{3,2,1,0:T(8,128)S(1)}, /*index=5*/f32[3,8,8,64]{3,2,1,0:T(8,128)S(1)}, s32[]{:T(128)}) while((s32[]{:T(128)}, f32[3,8,8,64]{3,2,1,0:T(8,128)S(1)}, pred[]{:T(512)}, f32[10,10,64]{2,1,0:T(8,128)S(1)}, ...), condition=%wide.region_4.5_spmd, body=%wide.region_3.4_spmd.sunk | while | flops 233730 | bytes 2351254 | solution.py:104
  193.5 5.2 collective-permute-start.4
  198.7 5.0 collective-permute-done.4
  207.4 4.2 collective-permute-done.1
  220.7 6.1 %collective-permute-done.4 = f32[3,8,8,64]{3,2,1,0:T(8,128)S(1)} collective-permute-done((f32[3,8,8,64]{3,2,1,0:T(8,128)S(1)}, f32[3,8,8,64]{3,2,1,0:T(8,128)S(1)}, u32[]{:S(2)}, u32[]{:S(2)}) %collective-permute-start.4) | collective-permute-done | bytes 49184 | tf_op jit(solution)/shard_map/while/body/eval_jaxpr/ppermute | solution.py:25
  235.7 4.7 collective-permute-start.3
  244.3 7.0 %collective-permute-done.4 = f32[3,8,8,64]{3,2,1,0:T(8,128)S(1)} collective-permute-done((f32[3,8,8,64]{3,2,1,0:T(8,128)S(1)}, f32[3,8,8,64]{3,2,1,0:T(8,128)S(1)}, u32[]{:S(2)}, u32[]{:S(2)}) %collective-permute-start.4) | collective-permute-done | bytes 49184 | tf_op jit(solution)/shard_map/while/body/eval_jaxpr/ppermute | solution.py:25
  268.1 7.5 %collective-permute-done.4 = f32[3,8,8,64]{3,2,1,0:T(8,128)S(1)} collective-permute-done((f32[3,8,8,64]{3,2,1,0:T(8,128)S(1)}, f32[3,8,8,64]{3,2,1,0:T(8,128)S(1)}, u32[]{:S(2)}, u32[]{:S(2)}) %collective-permute-start.4) | collective-permute-done | bytes 49184 | tf_op jit(solution)/shard_map/while/body/eval_jaxpr/ppermute | solution.py:25
  284.7 5.7 collective-permute-start.3
  293.8 8.5 %collective-permute-done.4 = f32[3,8,8,64]{3,2,1,0:T(8,128)S(1)} collective-permute-done((f32[3,8,8,64]{3,2,1,0:T(8,128)S(1)}, f32[3,8,8,64]{3,2,1,0:T(8,128)S(1)}, u32[]{:S(2)}, u32[]{:S(2)}) %collective-permute-start.4) | collective-permute-done | bytes 49184 | tf_op jit(solution)/shard_map/while/body/eval_jaxpr/ppermute | solution.py:25
  318.2 8.5 %collective-permute-done.4 = f32[3,8,8,64]{3,2,1,0:T(8,128)S(1)} collective-permute-done((f32[3,8,8,64]{3,2,1,0:T(8,128)S(1)}, f32[3,8,8,64]{3,2,1,0:T(8,128)S(1)}, u32[]{:S(2)}, u32[]{:S(2)}) %collective-permute-start.4) | collective-permute-done | bytes 49184 | tf_op jit(solution)/shard_map/while/body/eval_jaxpr/ppermute | solution.py:25
  342.6 8.5 %collective-permute-done.4 = f32[3,8,8,64]{3,2,1,0:T(8,128)S(1)} collective-permute-done((f32[3,8,8,64]{3,2,1,0:T(8,128)S(1)}, f32[3,8,8,64]{3,2,1,0:T(8,128)S(1)}, u32[]{:S(2)}, u32[]{:S(2)}) %collective-permute-start.4) | collective-permute-done | bytes 49184 | tf_op jit(solution)/shard_map/while/body/eval_jaxpr/ppermute | solution.py:25
  367.4 8.5 %collective-permute-done.4 = f32[3,8,8,64]{3,2,1,0:T(8,128)S(1)} collective-permute-done((f32[3,8,8,64]{3,2,1,0:T(8,128)S(1)}, f32[3,8,8,64]{3,2,1,0:T(8,128)S(1)}, u32[]{:S(2)}, u32[]{:S(2)}) %collective-permute-start.4) | collective-permute-done | bytes 49184 | tf_op jit(solution)/shard_map/while/body/eval_jaxpr/ppermute | solution.py:25
  392.2 8.6 %collective-permute-done.4 = f32[3,8,8,64]{3,2,1,0:T(8,128)S(1)} collective-permute-done((f32[3,8,8,64]{3,2,1,0:T(8,128)S(1)}, f32[3,8,8,64]{3,2,1,0:T(8,128)S(1)}, u32[]{:S(2)}, u32[]{:S(2)}) %collective-permute-start.4) | collective-permute-done | bytes 49184 | tf_op jit(solution)/shard_map/while/body/eval_jaxpr/ppermute | solution.py:25
  417.0 8.6 %collective-permute-done.4 = f32[3,8,8,64]{3,2,1,0:T(8,128)S(1)} collective-permute-done((f32[3,8,8,64]{3,2,1,0:T(8,128)S(1)}, f32[3,8,8,64]{3,2,1,0:T(8,128)S(1)}, u32[]{:S(2)}, u32[]{:S(2)}) %collective-permute-start.4) | collective-permute-done | bytes 49184 | tf_op jit(solution)/shard_map/while/body/eval_jaxpr/ppermute | solution.py:25
  441.8 8.6 %collective-permute-done.4 = f32[3,8,8,64]{3,2,1,0:T(8,128)S(1)} collective-permute-done((f32[3,8,8,64]{3,2,1,0:T(8,128)S(1)}, f32[3,8,8,64]{3,2,1,0:T(8,128)S(1)}, u32[]{:S(2)}, u32[]{:S(2)}) %collective-permute-start.4) | collective-permute-done | bytes 49184 | tf_op jit(solution)/shard_map/while/body/eval_jaxpr/ppermute | solution.py:25
  466.7 8.6 %collective-permute-done.4 = f32[3,8,8,64]{3,2,1,0:T(8,128)S(1)} collective-permute-done((f32[3,8,8,64]{3,2,1,0:T(8,128)S(1)}, f32[3,8,8,64]{3,2,1,0:T(8,128)S(1)}, u32[]{:S(2)}, u32[]{:S(2)}) %collective-permute-start.4) | collective-permute-done | bytes 49184 | tf_op jit(solution)/shard_map/while/body/eval_jaxpr/ppermute | solution.py:25
  491.5 8.5 %collective-permute-done.4 = f32[3,8,8,64]{3,2,1,0:T(8,128)S(1)} collective-permute-done((f32[3,8,8,64]{3,2,1,0:T(8,128)S(1)}, f32[3,8,8,64]{3,2,1,0:T(8,128)S(1)}, u32[]{:S(2)}, u32[]{:S(2)}) %collective-permute-start.4) | collective-permute-done | bytes 49184 | tf_op jit(solution)/shard_map/while/body/eval_jaxpr/ppermute | solution.py:25
  516.3 8.5 %collective-permute-done.4 = f32[3,8,8,64]{3,2,1,0:T(8,128)S(1)} collective-permute-done((f32[3,8,8,64]{3,2,1,0:T(8,128)S(1)}, f32[3,8,8,64]{3,2,1,0:T(8,128)S(1)}, u32[]{:S(2)}, u32[]{:S(2)}) %collective-permute-start.4) | collective-permute-done | bytes 49184 | tf_op jit(solution)/shard_map/while/body/eval_jaxpr/ppermute | solution.py:25
  541.1 8.5 %collective-permute-done.4 = f32[3,8,8,64]{3,2,1,0:T(8,128)S(1)} collective-permute-done((f32[3,8,8,64]{3,2,1,0:T(8,128)S(1)}, f32[3,8,8,64]{3,2,1,0:T(8,128)S(1)}, u32[]{:S(2)}, u32[]{:S(2)}) %collective-permute-start.4) | collective-permute-done | bytes 49184 | tf_op jit(solution)/shard_map/while/body/eval_jaxpr/ppermute | solution.py:25
  564.3 4.6 collective-permute-done.28
  (606 shorter events, 313.4 us)
Async XLA Ops:
  36.8 35.5 %collective-permute-start.21 = (f32[3,1,8,64]{3,2,1,0:T(8,128)S(1)}, f32[3,1,8,64]{3,2,1,0:T(8,128)S(1)}, u32[]{:S(2)}, u32[]{:S(2)}) collective-permute-start(f32[3,1,8,64]{3,2,1,0:T(8,128)S(1)} %get-tuple-element.234), channel_id=1, source_target_pairs={{0,4},{4,8},{8,12},{1,5},{5,9},{9,13},{2,6},{6,10},{10,14},{3,7},{... | collective-permute-start | bytes 18440 | tf_op jit(solution)/shard_map/ppermute | solution.py:16
  40.2 32.1 %collective-permute-start.22 = (f32[3,1,8,64]{3,2,1,0:T(8,128)S(1)}, f32[3,1,8,64]{3,2,1,0:T(8,128)S(1)}, u32[]{:S(2)}, u32[]{:S(2)}) collective-permute-start(f32[3,1,8,64]{3,2,1,0:T(8,128)S(1)} %get-tuple-element.235), channel_id=1, source_target_pairs={{4,0},{8,4},{12,8},{5,1},{9,5},{13,9},{6,2},{10,6},{14,10},{7,3},{... | collective-permute-start | bytes 18440 | tf_op jit(solution)/shard_map/ppermute | solution.py:17
  41.6 37.4 %collective-permute-start.5 = (f32[3,1,16,128]{3,2,1,0:T(8,128)S(1)}, f32[3,1,16,128]{3,2,1,0:T(8,128)S(1)}, u32[]{:S(2)}, u32[]{:S(2)}) collective-permute-start(f32[3,1,16,128]{3,2,1,0:T(8,128)S(1)} %get-tuple-element.198), channel_id=1, source_target_pairs={{0,4},{4,8},{8,12},{1,5},{5,9},{9,13},{2,6},{6,10},{10,14},{3,7},{... | collective-permute-start | bytes 73736 | tf_op jit(solution)/shard_map/ppermute | solution.py:16
  46.1 32.9 %collective-permute-start.6 = (f32[3,1,16,128]{3,2,1,0:T(8,128)S(1)}, f32[3,1,16,128]{3,2,1,0:T(8,128)S(1)}, u32[]{:S(2)}, u32[]{:S(2)}) collective-permute-start(f32[3,1,16,128]{3,2,1,0:T(8,128)S(1)} %get-tuple-element.199), channel_id=1, source_target_pairs={{4,0},{8,4},{12,8},{5,1},{9,5},{13,9},{6,2},{10,6},{14,10},{7,3},{... | collective-permute-start | bytes 73736 | tf_op jit(solution)/shard_map/ppermute | solution.py:17
  72.4 5.9 %collective-permute-start.23 = (f32[3,10,1,64]{3,2,1,0:T(1,128)S(1)}, f32[3,10,1,64]{3,2,1,0:T(1,128)S(1)}, u32[]{:S(2)}, u32[]{:S(2)}) collective-permute-start(f32[3,10,1,64]{3,2,1,0:T(1,128)S(1)} %get-tuple-element.230), channel_id=1, source_target_pairs={{0,1},{1,2},{2,3},{4,5},{5,6},{6,7},{8,9},{9,10},{10,11},{12,13},{... | collective-permute-start | bytes 23048 | tf_op jit(solution)/shard_map/ppermute | solution.py:16
  79.1 5.9 %collective-permute-start.7 = (f32[3,18,1,128]{3,2,1,0:T(1,128)S(1)}, f32[3,18,1,128]{3,2,1,0:T(1,128)S(1)}, u32[]{:S(2)}, u32[]{:S(2)}) collective-permute-start(f32[3,18,1,128]{3,2,1,0:T(1,128)S(1)} %get-tuple-element.196), channel_id=1, source_target_pairs={{0,1},{1,2},{2,3},{4,5},{5,6},{6,7},{8,9},{9,10},{10,11},{12,13},{... | collective-permute-start | bytes 82952 | tf_op jit(solution)/shard_map/ppermute | solution.py:16
  89.2 6.5 %collective-permute-start.10 = (f32[3,1,16,128]{3,2,1,0:T(8,128)S(1)}, f32[3,1,16,128]{3,2,1,0:T(8,128)S(1)}, u32[]{:S(2)}, u32[]{:S(2)}) collective-permute-start(f32[3,1,16,128]{3,2,1,0:T(8,128)S(1)} %get-tuple-element.181), channel_id=1, source_target_pairs={{4,0},{8,4},{12,8},{5,1},{9,5},{13,9},{6,2},{10,6},{14,10},{7,3},{... | collective-permute-start | bytes 73736 | tf_op jit(solution)/shard_map/ppermute | solution.py:17
  90.5 6.7 %collective-permute-start.9 = (f32[3,1,16,128]{3,2,1,0:T(8,128)S(1)}, f32[3,1,16,128]{3,2,1,0:T(8,128)S(1)}, u32[]{:S(2)}, u32[]{:S(2)}) collective-permute-start(f32[3,1,16,128]{3,2,1,0:T(8,128)S(1)} %get-tuple-element.180), channel_id=1, source_target_pairs={{0,4},{4,8},{8,12},{1,5},{5,9},{9,13},{2,6},{6,10},{10,14},{3,7},{... | collective-permute-start | bytes 73736 | tf_op jit(solution)/shard_map/ppermute | solution.py:16
  105.6 5.7 collective-permute-start.13
  109.8 5.7 collective-permute-start.14
  127.8 5.7 collective-permute-start.18
  193.5 10.2 %collective-permute-start.4 = (f32[3,8,8,64]{3,2,1,0:T(8,128)S(1)}, f32[3,8,8,64]{3,2,1,0:T(8,128)S(1)}, u32[]{:S(2)}, u32[]{:S(2)}) collective-permute-start(f32[3,8,8,64]{3,2,1,0:T(8,128)S(1)} %fusion.33), channel_id=1, source_target_pairs={{0,16},{16,32},{32,48},{48,64},{64,80},{80,96},{96,112},{112,128},... | collective-permute-start | bytes 147464 | tf_op jit(solution)/shard_map/while/body/eval_jaxpr/ppermute | solution.py:25
  206.0 5.6 collective-permute-start.1
  217.3 9.5 %collective-permute-start.4 = (f32[3,8,8,64]{3,2,1,0:T(8,128)S(1)}, f32[3,8,8,64]{3,2,1,0:T(8,128)S(1)}, u32[]{:S(2)}, u32[]{:S(2)}) collective-permute-start(f32[3,8,8,64]{3,2,1,0:T(8,128)S(1)} %fusion.33), channel_id=1, source_target_pairs={{0,16},{16,32},{32,48},{48,64},{64,80},{80,96},{96,112},{112,128},... | collective-permute-start | bytes 147464 | tf_op jit(solution)/shard_map/while/body/eval_jaxpr/ppermute | solution.py:25
  234.4 6.0 %collective-permute-start.2 = (f32[3,10,1,64]{3,2,1,0:T(1,128)S(1)}, f32[3,10,1,64]{3,2,1,0:T(1,128)S(1)}, u32[]{:S(2)}, u32[]{:S(2)}) collective-permute-start(f32[3,10,1,64]{3,2,1,0:T(1,128)S(1)} %get-tuple-element.318), channel_id=1, source_target_pairs={{1,0},{2,1},{3,2},{5,4},{6,5},{7,6},{9,8},{10,9},{11,10},{13,12},{... | collective-permute-start | bytes 23048 | tf_op jit(solution)/shard_map/while/body/eval_jaxpr/ppermute | solution.py:17
  241.9 9.5 %collective-permute-start.4 = (f32[3,8,8,64]{3,2,1,0:T(8,128)S(1)}, f32[3,8,8,64]{3,2,1,0:T(8,128)S(1)}, u32[]{:S(2)}, u32[]{:S(2)}) collective-permute-start(f32[3,8,8,64]{3,2,1,0:T(8,128)S(1)} %fusion.33), channel_id=1, source_target_pairs={{0,16},{16,32},{32,48},{48,64},{64,80},{80,96},{96,112},{112,128},... | collective-permute-start | bytes 147464 | tf_op jit(solution)/shard_map/while/body/eval_jaxpr/ppermute | solution.py:25
  266.0 9.5 %collective-permute-start.4 = (f32[3,8,8,64]{3,2,1,0:T(8,128)S(1)}, f32[3,8,8,64]{3,2,1,0:T(8,128)S(1)}, u32[]{:S(2)}, u32[]{:S(2)}) collective-permute-start(f32[3,8,8,64]{3,2,1,0:T(8,128)S(1)} %fusion.33), channel_id=1, source_target_pairs={{0,16},{16,32},{32,48},{48,64},{64,80},{80,96},{96,112},{112,128},... | collective-permute-start | bytes 147464 | tf_op jit(solution)/shard_map/while/body/eval_jaxpr/ppermute | solution.py:25
  283.4 7.1 %collective-permute-start.2 = (f32[3,10,1,64]{3,2,1,0:T(1,128)S(1)}, f32[3,10,1,64]{3,2,1,0:T(1,128)S(1)}, u32[]{:S(2)}, u32[]{:S(2)}) collective-permute-start(f32[3,10,1,64]{3,2,1,0:T(1,128)S(1)} %get-tuple-element.318), channel_id=1, source_target_pairs={{1,0},{2,1},{3,2},{5,4},{6,5},{7,6},{9,8},{10,9},{11,10},{13,12},{... | collective-permute-start | bytes 23048 | tf_op jit(solution)/shard_map/while/body/eval_jaxpr/ppermute | solution.py:17
  284.7 6.6 %collective-permute-start.3 = (f32[3,10,1,64]{3,2,1,0:T(1,128)S(1)}, f32[3,10,1,64]{3,2,1,0:T(1,128)S(1)}, u32[]{:S(2)}, u32[]{:S(2)}) collective-permute-start(f32[3,10,1,64]{3,2,1,0:T(1,128)S(1)} %get-tuple-element.319), channel_id=1, source_target_pairs={{0,1},{1,2},{2,3},{4,5},{5,6},{6,7},{8,9},{9,10},{10,11},{12,13},{... | collective-permute-start | bytes 23048 | tf_op jit(solution)/shard_map/while/body/eval_jaxpr/ppermute | solution.py:16
  291.9 10.4 %collective-permute-start.4 = (f32[3,8,8,64]{3,2,1,0:T(8,128)S(1)}, f32[3,8,8,64]{3,2,1,0:T(8,128)S(1)}, u32[]{:S(2)}, u32[]{:S(2)}) collective-permute-start(f32[3,8,8,64]{3,2,1,0:T(8,128)S(1)} %fusion.33), channel_id=1, source_target_pairs={{0,16},{16,32},{32,48},{48,64},{64,80},{80,96},{96,112},{112,128},... | collective-permute-start | bytes 147464 | tf_op jit(solution)/shard_map/while/body/eval_jaxpr/ppermute | solution.py:25
  316.3 10.4 %collective-permute-start.4 = (f32[3,8,8,64]{3,2,1,0:T(8,128)S(1)}, f32[3,8,8,64]{3,2,1,0:T(8,128)S(1)}, u32[]{:S(2)}, u32[]{:S(2)}) collective-permute-start(f32[3,8,8,64]{3,2,1,0:T(8,128)S(1)} %fusion.33), channel_id=1, source_target_pairs={{0,16},{16,32},{32,48},{48,64},{64,80},{80,96},{96,112},{112,128},... | collective-permute-start | bytes 147464 | tf_op jit(solution)/shard_map/while/body/eval_jaxpr/ppermute | solution.py:25
  340.7 10.4 %collective-permute-start.4 = (f32[3,8,8,64]{3,2,1,0:T(8,128)S(1)}, f32[3,8,8,64]{3,2,1,0:T(8,128)S(1)}, u32[]{:S(2)}, u32[]{:S(2)}) collective-permute-start(f32[3,8,8,64]{3,2,1,0:T(8,128)S(1)} %fusion.33), channel_id=1, source_target_pairs={{0,16},{16,32},{32,48},{48,64},{64,80},{80,96},{96,112},{112,128},... | collective-permute-start | bytes 147464 | tf_op jit(solution)/shard_map/while/body/eval_jaxpr/ppermute | solution.py:25
  365.5 10.4 %collective-permute-start.4 = (f32[3,8,8,64]{3,2,1,0:T(8,128)S(1)}, f32[3,8,8,64]{3,2,1,0:T(8,128)S(1)}, u32[]{:S(2)}, u32[]{:S(2)}) collective-permute-start(f32[3,8,8,64]{3,2,1,0:T(8,128)S(1)} %fusion.33), channel_id=1, source_target_pairs={{0,16},{16,32},{32,48},{48,64},{64,80},{80,96},{96,112},{112,128},... | collective-permute-start | bytes 147464 | tf_op jit(solution)/shard_map/while/body/eval_jaxpr/ppermute | solution.py:25
  390.3 10.6 %collective-permute-start.4 = (f32[3,8,8,64]{3,2,1,0:T(8,128)S(1)}, f32[3,8,8,64]{3,2,1,0:T(8,128)S(1)}, u32[]{:S(2)}, u32[]{:S(2)}) collective-permute-start(f32[3,8,8,64]{3,2,1,0:T(8,128)S(1)} %fusion.33), channel_id=1, source_target_pairs={{0,16},{16,32},{32,48},{48,64},{64,80},{80,96},{96,112},{112,128},... | collective-permute-start | bytes 147464 | tf_op jit(solution)/shard_map/while/body/eval_jaxpr/ppermute | solution.py:25
  415.1 10.6 %collective-permute-start.4 = (f32[3,8,8,64]{3,2,1,0:T(8,128)S(1)}, f32[3,8,8,64]{3,2,1,0:T(8,128)S(1)}, u32[]{:S(2)}, u32[]{:S(2)}) collective-permute-start(f32[3,8,8,64]{3,2,1,0:T(8,128)S(1)} %fusion.33), channel_id=1, source_target_pairs={{0,16},{16,32},{32,48},{48,64},{64,80},{80,96},{96,112},{112,128},... | collective-permute-start | bytes 147464 | tf_op jit(solution)/shard_map/while/body/eval_jaxpr/ppermute | solution.py:25
  439.8 10.6 %collective-permute-start.4 = (f32[3,8,8,64]{3,2,1,0:T(8,128)S(1)}, f32[3,8,8,64]{3,2,1,0:T(8,128)S(1)}, u32[]{:S(2)}, u32[]{:S(2)}) collective-permute-start(f32[3,8,8,64]{3,2,1,0:T(8,128)S(1)} %fusion.33), channel_id=1, source_target_pairs={{0,16},{16,32},{32,48},{48,64},{64,80},{80,96},{96,112},{112,128},... | collective-permute-start | bytes 147464 | tf_op jit(solution)/shard_map/while/body/eval_jaxpr/ppermute | solution.py:25
  464.8 10.5 %collective-permute-start.4 = (f32[3,8,8,64]{3,2,1,0:T(8,128)S(1)}, f32[3,8,8,64]{3,2,1,0:T(8,128)S(1)}, u32[]{:S(2)}, u32[]{:S(2)}) collective-permute-start(f32[3,8,8,64]{3,2,1,0:T(8,128)S(1)} %fusion.33), channel_id=1, source_target_pairs={{0,16},{16,32},{32,48},{48,64},{64,80},{80,96},{96,112},{112,128},... | collective-permute-start | bytes 147464 | tf_op jit(solution)/shard_map/while/body/eval_jaxpr/ppermute | solution.py:25
  489.6 10.5 %collective-permute-start.4 = (f32[3,8,8,64]{3,2,1,0:T(8,128)S(1)}, f32[3,8,8,64]{3,2,1,0:T(8,128)S(1)}, u32[]{:S(2)}, u32[]{:S(2)}) collective-permute-start(f32[3,8,8,64]{3,2,1,0:T(8,128)S(1)} %fusion.33), channel_id=1, source_target_pairs={{0,16},{16,32},{32,48},{48,64},{64,80},{80,96},{96,112},{112,128},... | collective-permute-start | bytes 147464 | tf_op jit(solution)/shard_map/while/body/eval_jaxpr/ppermute | solution.py:25
  514.4 10.5 %collective-permute-start.4 = (f32[3,8,8,64]{3,2,1,0:T(8,128)S(1)}, f32[3,8,8,64]{3,2,1,0:T(8,128)S(1)}, u32[]{:S(2)}, u32[]{:S(2)}) collective-permute-start(f32[3,8,8,64]{3,2,1,0:T(8,128)S(1)} %fusion.33), channel_id=1, source_target_pairs={{0,16},{16,32},{32,48},{48,64},{64,80},{80,96},{96,112},{112,128},... | collective-permute-start | bytes 147464 | tf_op jit(solution)/shard_map/while/body/eval_jaxpr/ppermute | solution.py:25
  539.2 10.5 %collective-permute-start.4 = (f32[3,8,8,64]{3,2,1,0:T(8,128)S(1)}, f32[3,8,8,64]{3,2,1,0:T(8,128)S(1)}, u32[]{:S(2)}, u32[]{:S(2)}) collective-permute-start(f32[3,8,8,64]{3,2,1,0:T(8,128)S(1)} %fusion.33), channel_id=1, source_target_pairs={{0,16},{16,32},{32,48},{48,64},{64,80},{80,96},{96,112},{112,128},... | collective-permute-start | bytes 147464 | tf_op jit(solution)/shard_map/while/body/eval_jaxpr/ppermute | solution.py:25
  557.9 6.4 %collective-permute-start.27 = (f32[3,10,1,64]{3,2,1,0:T(1,128)}, f32[3,10,1,64]{3,2,1,0:T(1,128)}, u32[]{:S(2)}, u32[]{:S(2)}) collective-permute-start(f32[3,10,1,64]{3,2,1,0:T(1,128)} %get-tuple-element.228), channel_id=1, source_target_pairs={{0,1},{1,2},{2,3},{4,5},{5,6},{6,7},{8,9},{9,10},{10,11},{12,13},{... | collective-permute-start | bytes 23048 | tf_op jit(solution)/shard_map/ppermute | solution.py:16
  561.8 7.1 %collective-permute-start.28 = (f32[3,10,1,64]{3,2,1,0:T(1,128)}, f32[3,10,1,64]{3,2,1,0:T(1,128)}, u32[]{:S(2)}, u32[]{:S(2)}) collective-permute-start(f32[3,10,1,64]{3,2,1,0:T(1,128)} %get-tuple-element.229), channel_id=1, source_target_pairs={{1,0},{2,1},{3,2},{5,4},{6,5},{7,6},{9,8},{10,9},{11,10},{13,12},{... | collective-permute-start | bytes 23048 | tf_op jit(solution)/shard_map/ppermute | solution.py:17
  (76 other events, 518.7 us)
where the time goes:
time: 585 us; the launch traced here: 579 us
  waiting for transfers between devices  225 us (38%)
  starting transfers between devices  224 us (38%)
  local copies, waits for them, and re-layouts  78.9 us (13%)
  other arithmetic  45.6 us (8%)
    ppermute x42, starting transfers between devices, padded(): before = lax.ppermute(last, axis, up)  135 us
    ppermute x15, waiting for transfers between devices, passed_along(): lax.ppermute(value, axis, [(source, source + steps) for source in range(f...  120 us
    ppermute x42, waiting for transfers between devices, padded(): after = lax.ppermute(first, axis, down)  90.5 us
    ppermute x42, starting transfers between devices, padded(): after = lax.ppermute(first, axis, down)  54.4 us
    another operation x2, local copies, waits for them, and re-layouts, restrict(): field.reshape(comps, size_a // 2, 2, size_b // 2, 2, size_c // 2, 2)  37.1 us
    ppermute x15, starting transfers between devices, passed_along(): lax.ppermute(value, axis, [(source, source + steps) for source in range(f...  34.2 us
    reshape x1, local copies, waits for them, and re-layouts, restrict(): field.reshape(comps, size_a // 2, 2, size_b // 2, 2, size_c // 2, 2)  26.6 us
    reduce_sum x3, other arithmetic, restrict(): return jnp.mean(blocks, axis=(2, 4, 6))  23 us
  transfers between devices with their start and end apart: 99, of which 73 were waited for; matrix products, arithmetic and copies ran while one was open for 5% of the time, Pallas kernels for 0%

commit v1 on v0

v1 whole, which is shorter than its diff:
```python
import jax
import jax.numpy as jnp
from jax import lax
from jax.experimental import pallas as pl
from jax.experimental.pallas import tpu as pltpu
from jax.sharding import PartitionSpec as P

DT = 0.015
MESH = pl.DeviceIdType.MESH
HIGHEST = lax.Precision.HIGHEST
DIRS = [(di, dj) for di in (-1, 0, 1) for dj in (-1, 0, 1) if (di, dj) != (0, 0)]
F32 = jnp.float32


def shifts(rows, last):
    lane = lax.broadcasted_iota(jnp.int32, (rows, 128), 1)
    keep_up = lane < last
    keep_down = lane > 0

    def col_next(x):
        return pltpu.roll(x, rows - 1, 0)

    def col_prev(x):
        return pltpu.roll(x, 1, 0)

    def z_next(x):
        return jnp.where(keep_up, pltpu.roll(x, 127, 1), 0.0)

    def z_prev(x):
        return jnp.where(keep_down, pltpu.roll(x, 1, 1), 0.0)

    return col_next, col_prev, z_next, z_prev


def sweep(src, dst, low, high, last, finish):
    col_next, col_prev, z_next, z_prev = shifts(24, last)

    def twists(i):
        v0, v1, v2 = src[0, i], src[1, i], src[2, i]
        h1 = (z_next(v0) - v0) - (src[2, i + 1] - v2)
        h2 = (src[1, i + 1] - v1) - (col_next(v0) - v0)
        return v0, v1, v2, h1, h2

    def row(i, carry):
        h1_before, h2_before = carry
        v0, v1, v2, h1, h2 = twists(i)
        h0 = (col_next(v2) - v2) - (z_next(v1) - v1)
        k0 = (h2 - col_prev(h2)) - (h1 - z_prev(h1))
        k1 = (h0 - z_prev(h0)) - (h2 - h2_before)
        k2 = (h1 - h1_before) - (h0 - col_prev(h0))
        finish(dst, i, (v0, v1, v2), (k0, k1, k2))
        return h1, h2

    before = twists(low - 1)
    lax.fori_loop(low, high, row, (before[3], before[4]))


def restrict(read, comps, sums):
    for half in range(2):
        for c in range(comps):
            for k in range(4):
                i = 2 * (4 * half + k)
                sums[half, c, k] = (read(c, i, 0) + read(c, i, 1)) + (read(c, i + 1, 0) + read(c, i + 1, 1))
    z = lax.broadcasted_iota(jnp.int32, (128, 128), 0)
    lane = lax.broadcasted_iota(jnp.int32, (128, 128), 1)
    total = 0.0
    for half in range(2):
        pick = jnp.where(lane == z // 2 + 64 * half, 0.125, 0.0).astype(F32)
        x = sums[half, 0:comps].reshape(comps * 32, 128)
        total = total + jnp.dot(x, pick, precision=HIGHEST, preferred_element_type=F32)
    return total.reshape(comps, 4, 8, 128)


def kernel(
    state, wave, cond, layer, mask, out,
    w, v, near, far, lay, msk, sums, ck, exa, exb, rs, rs_next, ps, arrived, c0, c1, ckf, acc,
    in_sem, fine_send, fine_recv, ck_send, ck_recv, a_send, a_recv, b_send, b_recv, rs_send, rs_recv, p_send, p_recv,
):
    n, gx, gy = lax.axis_index("tm"), lax.axis_index("gx"), lax.axis_index("gy")
    slices = 16

    def beside(di, dj):
        return (n, lax.rem(gx + di + 4, 4), lax.rem(gy + dj + 4, 4))

    def remote(src, dst, ssem, rsem, device):
        return pltpu.make_async_remote_copy(
            src_ref=src, dst_ref=dst, send_sem=ssem, recv_sem=rsem, device_id=device, device_id_type=MESH
        )

    loads = [
        pltpu.make_async_copy(state.at[0], w.at[0:3, 4:20, 0:16], in_sem.at[0]),
        pltpu.make_async_copy(layer, lay, in_sem.at[1]),
        pltpu.make_async_copy(mask, msk, in_sem.at[2]),
    ]
    for load in loads:
        load.start()

    barrier = pltpu.get_barrier_semaphore()
    for di, dj in DIRS:
        pl.semaphore_signal(barrier, inc=1, device_id=beside(di, dj), device_id_type=MESH)
    for m in range(1, slices):
        pl.semaphore_signal(barrier, inc=1, device_id=(lax.rem(n + m, slices), gx, gy), device_id_type=MESH)

    for load in loads:
        load.wait()

    for i in range(16):
        chosen = jnp.full((16, 128), cond[0], F32)
        for level in range(1, 16):
            chosen = jnp.where(lay[i] == level, cond[level], chosen)
        scaled = DT / chosen
        w[3, 4 + i, 0:16] = scaled
        w[4, 4 + i, 0:16] = scaled * msk[i].astype(F32)
    near[0] = w[:, 4:20, 0:4]
    near[1] = w[:, 4:20, 12:16]

    pl.semaphore_wait(barrier, len(DIRS) + slices - 1)

    def fine_ends(di, dj):
        if dj == 0:
            return (w.at[:, 4:8, 0:16], w.at[:, 20:24, 0:16]) if di < 0 else (w.at[:, 16:20, 0:16], w.at[:, 0:4, 0:16])
        side = 0 if dj < 0 else 1
        if di == 0:
            return near.at[side], far.at[side, :, 4:20]
        if di < 0:
            return near.at[side, :, 0:4], far.at[side, :, 20:24]
        return near.at[side, :, 12:16], far.at[side, :, 0:4]

    fine_copies = []
    for k, (di, dj) in enumerate(DIRS):
        source, target = fine_ends(di, dj)
        copy = remote(source, target, fine_send.at[k], fine_recv.at[k], beside(di, dj))
        copy.start()
        fine_copies.append(copy)

    def exchange(buf, ssem, rsem):
        copies = []
        for k, (di, dj) in enumerate(DIRS):
            copy = remote(buf.at[1, 1], buf.at[1 - di, 1 - dj], ssem.at[k], rsem.at[k], beside(di, dj))
            copy.start()
            copies.append(copy)
        return copies

    ck[1, 1] = restrict(lambda c, i, b: w[3, 4 + i, pl.ds(b, 8, stride=2)], 1, sums)[0]
    ck_copies = exchange(ck, ck_send, ck_recv)
    rs[...] = restrict(lambda c, i, b: w[c, 4 + i, pl.ds(b, 8, stride=2)], 3, sums)
    rs_copy = remote(rs, rs_next, rs_send.at[0], rs_recv.at[0], (lax.rem(n + slices - 1, slices), gx, gy))
    rs_copy.start()

    for copy in fine_copies:
        copy.wait()

    inside = {
        (-1, 0): jnp.where(gx > 0, 1.0, 0.0).astype(F32),
        (1, 0): jnp.where(gx < 3, 1.0, 0.0).astype(F32),
        (0, -1): jnp.where(gy > 0, 1.0, 0.0).astype(F32),
        (0, 1): jnp.where(gy < 3, 1.0, 0.0).astype(F32),
    }
    for c in range(5):
        w[c, :, 16:20] = far[0, c] * inside[0, 1]
        w[c, :, 20:24] = far[1, c] * inside[0, -1]

    @pl.when(gx == 0)
    def _():
        w[:, 0:4] = jnp.zeros((5, 4, 24, 128), F32)

    @pl.when(gx == 3)
    def _():
        w[:, 20:24] = jnp.zeros((5, 4, 24, 128), F32)

    for step in range(4):
        pulse = wave[0, step]

        def finish(dst, i, values, curls, pulse=pulse):
            scaled = w[3, i]
            dst[0, i] = values[0] - scaled * curls[0] - pulse * w[4, i]
            dst[1, i] = values[1] - scaled * curls[1]
            dst[2, i] = values[2] - scaled * curls[2]

        src, dst = (w, v) if step % 2 == 0 else (v, w)
        sweep(src, dst, 1 + step, 23 - step, 127, finish)

    end = restrict(lambda c, i, b: w[c, 4 + i, pl.ds(b, 8, stride=2)], 3, sums)
    rs_copy.wait()
    exa[1, 1] = end - rs_next[...]
    a_copies = exchange(exa, a_send, a_recv)

    def flag(ei, ej):
        value = 1.0
        if ei != 0:
            value = value * inside[ei, 0]
        if ej != 0:
            value = value * inside[0, ej]
        return value

    tiles = {0: 0, 1: 1, -1: 2}

    def spread(block, scale, put, ei, ej):
        block = block * scale
        put(8 + 8 * ei, tiles[ej], block)
        put(12 + 8 * ei, tiles[ej], pltpu.roll(block, 64, block.ndim - 1))

    for copy in ck_copies:
        copy.wait()
    for ei in (-1, 0, 1):
        for ej in (-1, 0, 1):

            def put_kappa(row, tile, block):
                ckf[row : row + 4, 8 * tile : 8 * tile + 8] = block

            spread(ck[ei + 1, ej + 1], flag(ei, ej), put_kappa, ei, ej)

    def unpack(buf):
        for ei in (-1, 0, 1):
            for ej in (-1, 0, 1):
                for c in range(3):

                    def put(row, tile, block, c=c):
                        c0[c, row : row + 4, 8 * tile : 8 * tile + 8] = block

                    spread(buf[ei + 1, ej + 1, c], flag(ei, ej), put, ei, ej)

    left_half = lax.broadcasted_iota(jnp.int32, (4, 8, 128), 2) < 64

    def finish_coarse(dst, i, values, curls):
        scaled = ckf[i]
        for c in range(3):
            dst[c, i] = values[c] - scaled * curls[c]

    def power(m):
        return remote(
            ps.at[m - 1], arrived.at[m - 1], p_send.at[m - 1], p_recv.at[m - 1], (lax.rem(n + m, slices), gx, gy)
        )

    def one(src, dst, local, m):
        sweep(src, dst, local, 24 - local, 63, finish_coarse)
        for c in range(3):
            ps[m - 1, c] = jnp.where(left_half, dst[c, 8:12, 0:8], pltpu.roll(dst[c, 12:16, 0:8], 64, 2))

        @pl.when(n + m < slices)
        def _():
            power(m).start()

    def phase(first):
        def two(t, carry):
            one(c0, c1, 2 * t + 1, first + 2 * t + 1)
            one(c1, c0, 2 * t + 2, first + 2 * t + 2)
            return carry

        lax.fori_loop(0, 4, two, 0)

    for copy in a_copies:
        copy.wait()
    unpack(exa)
    phase(0)
    exb[1, 1] = ps[7]
    b_copies = exchange(exb, b_send, b_recv)
    for copy in b_copies:
        copy.wait()
    unpack(exb)
    phase(8)

    acc[...] = jnp.zeros_like(acc)

    def gather(m, carry):
        @pl.when(m <= n)
        def _():
            power(m).wait_recv()
            acc[...] += arrived[m - 1]

        @pl.when(n + m < slices)
        def _():
            power(m).wait_send()

        return carry

    lax.fori_loop(1, slices, gather, 0)

    z = lax.broadcasted_iota(jnp.int32, (128, 128), 1)
    lane = lax.broadcasted_iota(jnp.int32, (128, 128), 0)
    packed = acc[...].reshape(96, 128)
    for half in range(2):
        pick = jnp.where(lane == z // 2 + 64 * half, 1.0, 0.0).astype(F32)
        wide = jnp.dot(packed, pick, precision=HIGHEST, preferred_element_type=F32).reshape(3, 4, 8, 128)
        for c in range(3):
            for k in range(4):
                for a in range(2):
                    i = 2 * (4 * half + k) + a
                    for b in range(2):
                        cells = pl.ds(b, 8, stride=2)
                        out[0, c, i, cells] = w[c, 4 + i, cells] + wide[c, k]


def body(state, waveform, conductivity, layer_map, loop_mask):
    any_space = pl.BlockSpec(memory_space=pl.ANY)
    smem = pl.BlockSpec(memory_space=pltpu.SMEM)
    vmem = lambda *shape: pltpu.VMEM(shape, F32)
    dma = lambda count: pltpu.SemaphoreType.DMA((count,))
    return pl.pallas_call(
        kernel,
        out_shape=jax.ShapeDtypeStruct(state.shape, F32),
        in_specs=[any_space, smem, smem, any_space, any_space],
        out_specs=pl.BlockSpec(memory_space=pltpu.VMEM),
        scratch_shapes=[
            vmem(5, 24, 24, 128),
            vmem(3, 24, 24, 128),
            vmem(2, 5, 16, 4, 128),
            vmem(2, 5, 24, 4, 128),
            pltpu.VMEM((16, 16, 128), jnp.int32),
            pltpu.VMEM((16, 16, 128), jnp.int32),
            vmem(2, 3, 4, 8, 128),
            vmem(3, 3, 4, 8, 128),
            vmem(3, 3, 3, 4, 8, 128),
            vmem(3, 3, 3, 4, 8, 128),
            vmem(3, 4, 8, 128),
            vmem(3, 4, 8, 128),
            vmem(16, 3, 4, 8, 128),
            vmem(16, 3, 4, 8, 128),
            vmem(3, 24, 24, 128),
            vmem(3, 24, 24, 128),
            vmem(24, 24, 128),
            vmem(3, 4, 8, 128),
            dma(3),
            dma(8), dma(8), dma(8), dma(8), dma(8), dma(8), dma(8), dma(8),
            dma(1), dma(1), dma(16), dma(16),
        ],
        compiler_params=pltpu.CompilerParams(
            collective_id=0, has_side_effects=True, vmem_limit_bytes=40 * 1024 * 1024
        ),
        name="parareal",
    )(state, waveform, conductivity, layer_map, loop_mask)


def solution(mesh):
    placed = (
        P("tm", None, "gx", "gy", None),
        P("tm", None),
        P(),
        P("gx", "gy", None),
        P("gx", "gy", None),
    )
    return jax.shard_map(
        body, mesh=mesh, in_specs=placed, out_specs=P("tm", None, "gx", "gy", None), check_vma=False
    )
```

time: 585 us -> 92.3 us (0.16)
  the two profiles are of different devices: /device:TPU:24 before, /device:TPU:1 now
where the time goes in v1:
time: 92.3 us; the launch traced here: 92.1 us
  Pallas kernels  87.3 us (95%)
  local copies, waits for them, and re-layouts  4.86 us (5%)
    pallas_call x1, Pallas kernels, body(): pl.pallas_call(kernel, out_shape=jax.ShapeDtypeStruct(state.shape, F32),...  87.3 us
    unnamed x11, local copies, waits for them, and re-layouts  4.86 us

profile of v1, /device:TPU:1, one launch (start us, length us, event | category | flops | bytes accessed | tf_op | source)
XLA Modules:
  0.0 92.1 jit_solution(13444934037464978062)
XLA Ops:
  0.0 0.0 copy-start
  0.0 1.0 %copy-done = f32[1,3,16,16,128]{4,3,2,1,0:T(8,128)S(1)} copy-done((f32[1,3,16,16,128]{4,3,2,1,0:T(8,128)S(1)}, f32[1,3,16,16,128]{4,3,2,1,0:T(8,128)}, u32[]{:S(2)}) %copy-start) | copy-done | bytes 393240
  1.0 0.0 copy-start.1
  1.0 0.9 copy-done.1
  1.9 0.0 copy-start.2
  1.9 0.9 copy-done.2
  2.8 0.0 copy-start.3
  2.8 0.7 copy-done.3
  3.5 0.0 copy-start.4
  3.5 0.7 copy-done.4
  4.1 87.3 %parareal.1 = f32[1,3,16,16,128]{4,3,2,1,0:T(8,128)S(1)} custom-call(f32[1,3,16,16,128]{4,3,2,1,0:T(8,128)S(1)} %copy-done, f32[1,4]{1,0:T(1,128)S(1)} %copy-done.3, f32[16]{0:T(128)S(1)} %copy-done.4, s32[16,16,128]{2,1,0:T(8,128)S(1)} %copy-done.1, s32[16,16,128]{2,1,0:T(8,128)S(1)} %copy-done.2), custom_call_target="tpu_custom_call" | custom-call | tf_op jit(solution)/shard_map/parareal/pallas_call | solution.py:299
  91.4 0.7 copy.7
Async XLA Ops:
  0.0 1.0 %copy-start = (f32[1,3,16,16,128]{4,3,2,1,0:T(8,128)S(1)}, f32[1,3,16,16,128]{4,3,2,1,0:T(8,128)}, u32[]{:S(2)}) copy-start(f32[1,3,16,16,128]{4,3,2,1,0:T(8,128)} %state.1) | copy-start | bytes 1179652
  1.0 0.9 copy-start.1
  1.9 0.9 copy-start.2
  2.8 0.7 copy-start.3
  3.5 0.7 copy-start.4

commit v2 on v1

--- a/solution.py
+++ b/solution.py
@@ -6,6 +6,7 @@
 from jax.sharding import PartitionSpec as P
 
 DT = 0.015
+GROUP = 8
 MESH = pl.DeviceIdType.MESH
 HIGHEST = lax.Precision.HIGHEST
 DIRS = [(di, dj) for di in (-1, 0, 1) for dj in (-1, 0, 1) if (di, dj) != (0, 0)]
@@ -52,7 +53,17 @@
         return h1, h2
 
     before = twists(low - 1)
-    lax.fori_loop(low, high, row, (before[3], before[4]))
+    carry = (before[3], before[4])
+
+    def rows(t, carry):
+        for k in range(GROUP):
+            carry = row(low + GROUP * t + k, carry)
+        return carry
+
+    groups, rest = divmod(high - low, GROUP)
+    carry = lax.fori_loop(0, groups, rows, carry)
+    for k in range(rest):
+        carry = row(low + GROUP * groups + k, carry)
 
 
 def restrict(read, comps, sums):
@@ -73,14 +84,23 @@
 
 def kernel(
     state, wave, cond, layer, mask, out,
-    w, v, near, far, lay, msk, sums, ck, exa, exb, rs, rs_next, ps, arrived, c0, c1, ckf, acc,
+    w, v, near, far, lay, msk, sums, ck, exa, exb, rs, rs_next, ps, arrived, zs, zarr, c0, c1, ckf, acc,
     in_sem, fine_send, fine_recv, ck_send, ck_recv, a_send, a_recv, b_send, b_recv, rs_send, rs_recv, p_send, p_recv,
+    z_send, z_recv, linked,
 ):
     n, gx, gy = lax.axis_index("tm"), lax.axis_index("gx"), lax.axis_index("gy")
     slices = 16
 
+    plane, column = n // 4, lax.rem(n, 4)
+
     def beside(di, dj):
-        return (n, lax.rem(gx + di + 4, 4), lax.rem(gy + dj + 4, 4))
+        return (n, gx + di, gy + dj)
+
+    def exists(di, dj):
+        return (gx + di >= 0) & (gx + di < 4) & (gy + dj >= 0) & (gy + dj < 4)
+
+    def along(planes, columns):
+        return (4 * lax.rem(plane + planes + 4, 4) + lax.rem(column + columns + 4, 4), gx, gy)
 
     def remote(src, dst, ssem, rsem, device):
         return pltpu.make_async_remote_copy(
@@ -97,9 +117,35 @@
 
     barrier = pltpu.get_barrier_semaphore()
     for di, dj in DIRS:
-        pl.semaphore_signal(barrier, inc=1, device_id=beside(di, dj), device_id_type=MESH)
-    for m in range(1, slices):
-        pl.semaphore_signal(barrier, inc=1, device_id=(lax.rem(n + m, slices), gx, gy), device_id_type=MESH)
+
+        @pl.when(exists(di, dj))
+        def _(di=di, dj=dj):
+            pl.semaphore_signal(barrier, inc=1, device_id=beside(di, dj), device_id_type=MESH)
+
+    for planes, columns in ((1, 0), (2, 0), (3, 0), (0, 1), (0, 3)):
+        pl.semaphore_signal(barrier, inc=1, device_id=along(planes, columns), device_id_type=MESH)
+
+    @pl.when(gx == 0)
+    def _():
+        for buf in (ck, exa, exb):
+            buf[0] = jnp.zeros(buf.shape[1:], F32)
+
+    @pl.when(gx == 3)
+    def _():
+        for buf in (ck, exa, exb):
+            buf[2] = jnp.zeros(buf.shape[1:], F32)
+
+    @pl.when(gy == 0)
+    def _():
+        for buf in (ck, exa, exb):
+            buf[:, 0] = jnp.zeros((3,) + buf.shape[2:], F32)
+        far[1] = jnp.zeros(far.shape[1:], F32)
+
+    @pl.when(gy == 3)
+    def _():
+        for buf in (ck, exa, exb):
+            buf[:, 2] = jnp.zeros((3,) + buf.shape[2:], F32)
+        far[0] = jnp.zeros(far.shape[1:], F32)
 
     for load in loads:
         load.wait()
@@ -114,7 +160,11 @@
     near[0] = w[:, 4:20, 0:4]
     near[1] = w[:, 4:20, 12:16]
 
-    pl.semaphore_wait(barrier, len(DIRS) + slices - 1)
+    two, three = jnp.int32(2), jnp.int32(3)
+    in_x = jnp.where((gx == 0) | (gx == 3), two, three)
+    in_y = jnp.where((gy == 0) | (gy == 3), two, three)
+    pl.semaphore_wait(barrier, in_x * in_y - 1 + 5)
+    pl.semaphore_signal(linked, inc=1, device_id=along(0, 1), device_id_type=MESH)
 
     def fine_ends(di, dj):
         if dj == 0:
@@ -126,39 +176,37 @@
             return near.at[side, :, 0:4], far.at[side, :, 20:24]
         return near.at[side, :, 12:16], far.at[side, :, 0:4]
 
-    fine_copies = []
-    for k, (di, dj) in enumerate(DIRS):
-        source, target = fine_ends(di, dj)
-        copy = remote(source, target, fine_send.at[k], fine_recv.at[k], beside(di, dj))
-        copy.start()
-        fine_copies.append(copy)
-
-    def exchange(buf, ssem, rsem):
+    def swap(ends, ssem, rsem):
         copies = []
         for k, (di, dj) in enumerate(DIRS):
-            copy = remote(buf.at[1, 1], buf.at[1 - di, 1 - dj], ssem.at[k], rsem.at[k], beside(di, dj))
-            copy.start()
-            copies.append(copy)
-        return copies
-
+            source, target = ends(di, dj)
+            copy = remote(source, target, ssem.at[k], rsem.at[k], beside(di, dj))
+            pl.when(exists(di, dj))(copy.start)
+            copies.append((copy, di, dj))
+
+        def finish():
+            for copy, di, dj in copies:
+                pl.when(exists(-di, -dj))(copy.wait_recv)
+            for copy, di, dj in copies:
+                pl.when(exists(di, dj))(copy.wait_send)
+
+        return finish
+
+    def exchange(buf, ssem, rsem):
+        return swap(lambda di, dj: (buf.at[1, 1], buf.at[1 - di, 1 - dj]), ssem, rsem)
+
+    fine_arrive = swap(fine_ends, fine_send, fine_recv)
     ck[1, 1] = restrict(lambda c, i, b: w[3, 4 + i, pl.ds(b, 8, stride=2)], 1, sums)[0]
-    ck_copies = exchange(ck, ck_send, ck_recv)
+    ck_arrive = exchange(ck, ck_send, ck_recv)
     rs[...] = restrict(lambda c, i, b: w[c, 4 + i, pl.ds(b, 8, stride=2)], 3, sums)
     rs_copy = remote(rs, rs_next, rs_send.at[0], rs_recv.at[0], (lax.rem(n + slices - 1, slices), gx, gy))
-    rs_copy.start()
-
-    for copy in fine_copies:
-        copy.wait()
-
-    inside = {
-        (-1, 0): jnp.where(gx > 0, 1.0, 0.0).astype(F32),
-        (1, 0): jnp.where(gx < 3, 1.0, 0.0).astype(F32),
-        (0, -1): jnp.where(gy > 0, 1.0, 0.0).astype(F32),
-        (0, 1): jnp.where(gy < 3, 1.0, 0.0).astype(F32),
-    }
+    pl.semaphore_wait(linked, 1)
+    pl.when(n > 0)(rs_copy.start)
+
+    fine_arrive()
     for c in range(5):
-        w[c, :, 16:20] = far[0, c] * inside[0, 1]
-        w[c, :, 20:24] = far[1, c] * inside[0, -1]
+        w[c, :, 16:20] = far[0, c]
+        w[c, :, 20:24] = far[1, c]
 
     @pl.when(gx == 0)
     def _():
@@ -181,34 +229,25 @@
         sweep(src, dst, 1 + step, 23 - step, 127, finish)
 
     end = restrict(lambda c, i, b: w[c, 4 + i, pl.ds(b, 8, stride=2)], 3, sums)
-    rs_copy.wait()
+    pl.when(n < slices - 1)(rs_copy.wait_recv)
+    pl.when(n > 0)(rs_copy.wait_send)
     exa[1, 1] = end - rs_next[...]
-    a_copies = exchange(exa, a_send, a_recv)
-
-    def flag(ei, ej):
-        value = 1.0
-        if ei != 0:
-            value = value * inside[ei, 0]
-        if ej != 0:
-            value = value * inside[0, ej]
-        return value
+    a_arrive = exchange(exa, a_send, a_recv)
 
     tiles = {0: 0, 1: 1, -1: 2}
 
-    def spread(block, scale, put, ei, ej):
-        block = block * scale
+    def spread(block, put, ei, ej):
         put(8 + 8 * ei, tiles[ej], block)
         put(12 + 8 * ei, tiles[ej], pltpu.roll(block, 64, block.ndim - 1))
 
-    for copy in ck_copies:
-        copy.wait()
+    ck_arrive()
     for ei in (-1, 0, 1):
         for ej in (-1, 0, 1):
 
             def put_kappa(row, tile, block):
                 ckf[row : row + 4, 8 * tile : 8 * tile + 8] = block
 
-            spread(ck[ei + 1, ej + 1], flag(ei, ej), put_kappa, ei, ej)
+            spread(ck[ei + 1, ej + 1], put_kappa, ei, ej)
 
     def unpack(buf):
         for ei in (-1, 0, 1):
@@ -218,7 +257,7 @@
                     def put(row, tile, block, c=c):
                         c0[c, row : row + 4, 8 * tile : 8 * tile + 8] = block
 
-                    spread(buf[ei + 1, ej + 1, c], flag(ei, ej), put, ei, ej)
+                    spread(buf[ei + 1, ej + 1, c], put, ei, ej)
 
     left_half = lax.broadcasted_iota(jnp.int32, (4, 8, 128), 2) < 64
 
@@ -227,54 +266,85 @@
         for c in range(3):
             dst[c, i] = values[c] - scaled * curls[c]
 
+    def carried(b):
+        return jnp.where(column + b >= 4, jnp.int32(1), jnp.int32(0))
+
     def power(m):
-        return remote(
-            ps.at[m - 1], arrived.at[m - 1], p_send.at[m - 1], p_recv.at[m - 1], (lax.rem(n + m, slices), gx, gy)
-        )
+        planes = m // 4 + carried(m % 4)
+        copy = remote(ps.at[m - 1], arrived.at[m - 1], p_send.at[m - 1], p_recv.at[m - 1], along(planes, 0))
+        sent = (planes > 0) & (plane + planes < 4)
+        received = (planes > 0) & (plane - planes >= 0)
+        return copy, sent, received
 
     def one(src, dst, local, m):
         sweep(src, dst, local, 24 - local, 63, finish_coarse)
         for c in range(3):
             ps[m - 1, c] = jnp.where(left_half, dst[c, 8:12, 0:8], pltpu.roll(dst[c, 12:16, 0:8], 64, 2))
 
-        @pl.when(n + m < slices)
-        def _():
-            power(m).start()
+        copy, sent, _ = power(m)
+        pl.when(sent)(copy.start)
 
     def phase(first):
-        def two(t, carry):
-            one(c0, c1, 2 * t + 1, first + 2 * t + 1)
-            one(c1, c0, 2 * t + 2, first + 2 * t + 2)
-            return carry
-
-        lax.fori_loop(0, 4, two, 0)
-
-    for copy in a_copies:
-        copy.wait()
+        for step in range(1, 9):
+            if first + step < slices:
+                src, dst = (c0, c1) if step % 2 else (c1, c0)
+                one(src, dst, step, first + step)
+
+    a_arrive()
     unpack(exa)
     phase(0)
-    exb[1, 1] = ps[7]
-    b_copies = exchange(exb, b_send, b_recv)
-    for copy in b_copies:
-        copy.wait()
-    unpack(exb)
-    phase(8)
+
+    @pl.when(n < slices - 9)
+    def _():
+        exb[1, 1] = ps[7]
+        exchange(exb, b_send, b_recv)()
+        unpack(exb)
+        phase(8)
+
+    def across(b):
+        return remote(zs.at[b - 1], zarr.at[b - 1], z_send.at[b - 1], z_recv.at[b - 1], along(0, b))
+
+    for b in (1, 2, 3):
+        kept = plane >= carried(b)
+
+        @pl.when(carried(b) == 0)
+        def _(b=b):
+            zs[b - 1] = ps[b - 1]
+
+        @pl.when(carried(b) == 1)
+        def _(b=b):
+            zs[b - 1] = jnp.zeros(zs.shape[1:], F32)
+
+        for m in range(b, slices, 4):
+            copy, _, received = power(m)
+
+            @pl.when(received)
+            def _(copy=copy, m=m, b=b):
+                copy.wait_recv()
+                zs[b - 1] += arrived[m - 1]
+
+        pl.when(kept)(across(b).start)
 
     acc[...] = jnp.zeros_like(acc)
-
-    def gather(m, carry):
-        @pl.when(m <= n)
-        def _():
-            power(m).wait_recv()
+    for m in (4, 8, 12):
+        copy, _, received = power(m)
+
+        @pl.when(received)
+        def _(copy=copy, m=m):
+            copy.wait_recv()
             acc[...] += arrived[m - 1]
 
-        @pl.when(n + m < slices)
-        def _():
-            power(m).wait_send()
-
-        return carry
-
-    lax.fori_loop(1, slices, gather, 0)
+    for b in (1, 2, 3):
+        @pl.when((column >= b) | (plane > 0))
+        def _(b=b):
+            across(b).wait_recv()
+            acc[...] += zarr[b - 1]
+
+    for m in range(1, slices):
+        copy, sent, _ = power(m)
+        pl.when(sent)(copy.wait_send)
+    for b in (1, 2, 3):
+        pl.when(plane >= carried(b))(across(b).wait_send)
 
     z = lax.broadcasted_iota(jnp.int32, (128, 128), 1)
     lane = lax.broadcasted_iota(jnp.int32, (128, 128), 0)
@@ -316,16 +386,18 @@
             vmem(3, 4, 8, 128),
             vmem(16, 3, 4, 8, 128),
             vmem(16, 3, 4, 8, 128),
+            vmem(3, 3, 4, 8, 128),
+            vmem(3, 3, 4, 8, 128),
             vmem(3, 24, 24, 128),
             vmem(3, 24, 24, 128),
             vmem(24, 24, 128),
             vmem(3, 4, 8, 128),
             dma(3),
             dma(8), dma(8), dma(8), dma(8), dma(8), dma(8), dma(8), dma(8),
-            dma(1), dma(1), dma(16), dma(16),
+            dma(1), dma(1), dma(16), dma(16), dma(3), dma(3), pltpu.SemaphoreType.REGULAR,
         ],
         compiler_params=pltpu.CompilerParams(
-            collective_id=0, has_side_effects=True, vmem_limit_bytes=40 * 1024 * 1024
+            collective_id=0, has_side_effects=True, vmem_limit_bytes=60 * 1024 * 1024
         ),
         name="parareal",
     )(state, waveform, conductivity, layer_map, loop_mask)

time: 92.3 us -> 49.5 us (0.54)
  the two profiles are of different devices: /device:TPU:1 before, /device:TPU:24 now
where the time goes in v2:
time: 49.5 us; the launch traced here: 49.3 us
  Pallas kernels  47.6 us (96%)
  local copies, waits for them, and re-layouts  1.77 us (4%)
    pallas_call x1, Pallas kernels, body(): pl.pallas_call(kernel, out_shape=jax.ShapeDtypeStruct(state.shape, F32),...  47.6 us
    unnamed x1, local copies, waits for them, and re-layouts  1.77 us

profile of v2, /device:TPU:24, one launch (start us, length us, event | category | flops | bytes accessed | tf_op | source)
XLA Modules:
  0.0 49.3 jit_solution(459942266109076164)
XLA Ops:
  0.0 47.6 %parareal.1 = f32[1,3,16,16,128]{4,3,2,1,0:T(8,128)} custom-call(f32[1,3,16,16,128]{4,3,2,1,0:T(8,128)} %state.1, f32[1,4]{1,0:T(1,128)} %wave.1, f32[16]{0:T(128)} %cond.1, s32[16,16,128]{2,1,0:T(8,128)} %layer.1, s32[16,16,128]{2,1,0:T(8,128)} %mask.1), custom_call_target="tpu_custom_call" | custom-call | tf_op jit(solution)/shard_map/parareal/pallas_call | solution.py:369
  47.6 1.8 %copy.7 = f32[1,3,16,16,128]{4,3,2,1,0:T(8,128)} copy(f32[1,3,16,16,128]{4,3,2,1,0:T(8,128)} %parareal.1) | data formatting | bytes 786432

commit v3 on v2

--- a/solution.py
+++ b/solution.py
@@ -9,14 +9,14 @@
 GROUP = 8
 MESH = pl.DeviceIdType.MESH
 HIGHEST = lax.Precision.HIGHEST
-DIRS = [(di, dj) for di in (-1, 0, 1) for dj in (-1, 0, 1) if (di, dj) != (0, 0)]
+DIRS = [(-1, 0), (1, 0), (-1, -1), (1, 1), (-1, 1), (1, -1), (0, -1), (0, 1)]
 F32 = jnp.float32
 
 
-def shifts(rows, last):
-    lane = lax.broadcasted_iota(jnp.int32, (rows, 128), 1)
-    keep_up = lane < last
-    keep_down = lane > 0
+def shifts(rows, depth):
+    cell = lax.rem(lax.broadcasted_iota(jnp.int32, (rows, 128), 1), depth)
+    keep_up = cell < depth - 1
+    keep_down = cell > 0
 
     def col_next(x):
         return pltpu.roll(x, rows - 1, 0)
@@ -33,8 +33,8 @@
     return col_next, col_prev, z_next, z_prev
 
 
-def sweep(src, dst, low, high, last, finish):
-    col_next, col_prev, z_next, z_prev = shifts(24, last)
+def sweep(src, dst, low, high, finish):
+    col_next, col_prev, z_next, z_prev = shifts(24, 128)
 
     def twists(i):
         v0, v1, v2 = src[0, i], src[1, i], src[2, i]
@@ -66,11 +66,41 @@
         carry = row(low + GROUP * groups + k, carry)
 
 
+def folded_sweep(src, dst, low, finish):
+    col_next, col_prev, z_next, z_prev = shifts(24, 64)
+    left = lax.broadcasted_iota(jnp.int32, (24, 128), 1) < 64
+
+    def row_next(c, p, x):
+        after = src[c, p + 1] if p < 11 else pltpu.roll(x, 64, 1)
+        return jnp.where(left, after, src[c, p - 1] if p >= low else x)
+
+    def twists(p):
+        v0, v1, v2 = src[0, p], src[1, p], src[2, p]
+        h1 = (z_next(v0) - v0) - (row_next(2, p, v2) - v2)
+        h2 = (row_next(1, p, v1) - v1) - (col_next(v0) - v0)
+        return (v0, v1, v2), h1, h2
+
+    before, now = twists(low - 1), twists(low)
+    for p in range(low, 12):
+        values, h1, h2 = now
+        if p < 11:
+            after = twists(p + 1)
+        else:
+            after = (None, pltpu.roll(h1, 64, 1), pltpu.roll(h2, 64, 1))
+        v0, v1, v2 = values
+        h0 = (col_next(v2) - v2) - (z_next(v1) - v1)
+        k0 = (h2 - col_prev(h2)) - (h1 - z_prev(h1))
+        k1 = (h0 - z_prev(h0)) - (h2 - jnp.where(left, before[2], after[2]))
+        k2 = (h1 - jnp.where(left, before[1], after[1])) - (h0 - col_prev(h0))
+        finish(dst, p, values, (k0, k1, k2))
+        before, now = now, after
+
+
 def restrict(read, comps, sums):
     for half in range(2):
         for c in range(comps):
             for k in range(4):
-                i = 2 * (4 * half + k)
+                i = 2 * (7 - k if half else k)
                 sums[half, c, k] = (read(c, i, 0) + read(c, i, 1)) + (read(c, i + 1, 0) + read(c, i + 1, 1))
     z = lax.broadcasted_iota(jnp.int32, (128, 128), 0)
     lane = lax.broadcasted_iota(jnp.int32, (128, 128), 1)
@@ -164,7 +194,8 @@
     in_x = jnp.where((gx == 0) | (gx == 3), two, three)
     in_y = jnp.where((gy == 0) | (gy == 3), two, three)
     pl.semaphore_wait(barrier, in_x * in_y - 1 + 5)
-    pl.semaphore_signal(linked, inc=1, device_id=along(0, 1), device_id_type=MESH)
+    pl.semaphore_signal(linked.at[0], inc=1, device_id=along(0, 1), device_id_type=MESH)
+    pl.semaphore_signal(linked.at[1], inc=1, device_id=along(0, 3), device_id_type=MESH)
 
     def fine_ends(di, dj):
         if dj == 0:
@@ -180,9 +211,11 @@
         copies = []
         for k, (di, dj) in enumerate(DIRS):
             source, target = ends(di, dj)
-            copy = remote(source, target, ssem.at[k], rsem.at[k], beside(di, dj))
-            pl.when(exists(di, dj))(copy.start)
-            copies.append((copy, di, dj))
+            copies.append((remote(source, target, ssem.at[k], rsem.at[k], beside(di, dj)), di, dj))
+
+        def start():
+            for copy, di, dj in copies:
+                pl.when(exists(di, dj))(copy.start)
 
         def finish():
             for copy, di, dj in copies:
@@ -190,17 +223,20 @@
             for copy, di, dj in copies:
                 pl.when(exists(di, dj))(copy.wait_send)
 
-        return finish
+        return start, finish
 
     def exchange(buf, ssem, rsem):
         return swap(lambda di, dj: (buf.at[1, 1], buf.at[1 - di, 1 - dj]), ssem, rsem)
 
-    fine_arrive = swap(fine_ends, fine_send, fine_recv)
+    fine_start, fine_arrive = swap(fine_ends, fine_send, fine_recv)
+    fine_start()
     ck[1, 1] = restrict(lambda c, i, b: w[3, 4 + i, pl.ds(b, 8, stride=2)], 1, sums)[0]
-    ck_arrive = exchange(ck, ck_send, ck_recv)
+    ck_start, ck_arrive = exchange(ck, ck_send, ck_recv)
+    ck_start()
     rs[...] = restrict(lambda c, i, b: w[c, 4 + i, pl.ds(b, 8, stride=2)], 3, sums)
     rs_copy = remote(rs, rs_next, rs_send.at[0], rs_recv.at[0], (lax.rem(n + slices - 1, slices), gx, gy))
-    pl.semaphore_wait(linked, 1)
+    pl.semaphore_wait(linked.at[0], 1)
+    pl.semaphore_signal(linked.at[2], inc=1, device_id=along(0, 1), device_id_type=MESH)
     pl.when(n > 0)(rs_copy.start)
 
     fine_arrive()
@@ -226,40 +262,39 @@
             dst[2, i] = values[2] - scaled * curls[2]
 
         src, dst = (w, v) if step % 2 == 0 else (v, w)
-        sweep(src, dst, 1 + step, 23 - step, 127, finish)
+        sweep(src, dst, 1 + step, 23 - step, finish)
 
     end = restrict(lambda c, i, b: w[c, 4 + i, pl.ds(b, 8, stride=2)], 3, sums)
     pl.when(n < slices - 1)(rs_copy.wait_recv)
     pl.when(n > 0)(rs_copy.wait_send)
     exa[1, 1] = end - rs_next[...]
-    a_arrive = exchange(exa, a_send, a_recv)
-
-    tiles = {0: 0, 1: 1, -1: 2}
-
-    def spread(block, put, ei, ej):
-        put(8 + 8 * ei, tiles[ej], block)
-        put(12 + 8 * ei, tiles[ej], pltpu.roll(block, 64, block.ndim - 1))
+    a_start, a_arrive = exchange(exa, a_send, a_recv)
+    a_start()
+    b_start, b_arrive = exchange(exb, b_send, b_recv)
+
+    left_half = lax.broadcasted_iota(jnp.int32, (8, 128), 1) < 64
+
+    def fold(read, put):
+        for tile, ej in enumerate((0, 1, -1)):
+            for k in range(4):
+                up, down = read(-1, ej, k), read(1, ej, k)
+                put(k, tile, jnp.where(left_half, up, down))
+                put(7 - k, tile, pltpu.roll(jnp.where(left_half, down, up), 64, 1))
+                put(8 + k, tile, read(0, ej, k))
 
     ck_arrive()
-    for ei in (-1, 0, 1):
-        for ej in (-1, 0, 1):
-
-            def put_kappa(row, tile, block):
-                ckf[row : row + 4, 8 * tile : 8 * tile + 8] = block
-
-            spread(ck[ei + 1, ej + 1], put_kappa, ei, ej)
+    def put_kappa(row, tile, block):
+        ckf[row, 8 * tile : 8 * tile + 8] = block
+
+    fold(lambda ei, ej, k: ck[ei + 1, ej + 1, k], put_kappa)
 
     def unpack(buf):
-        for ei in (-1, 0, 1):
-            for ej in (-1, 0, 1):
-                for c in range(3):
-
-                    def put(row, tile, block, c=c):
-                        c0[c, row : row + 4, 8 * tile : 8 * tile + 8] = block
-
-                    spread(buf[ei + 1, ej + 1, c], put, ei, ej)
-
-    left_half = lax.broadcasted_iota(jnp.int32, (4, 8, 128), 2) < 64
+        for c in range(3):
+
+            def put(row, tile, block, c=c):
+                c0[c, row, 8 * tile : 8 * tile + 8] = block
+
+            fold(lambda ei, ej, k, c=c: buf[ei + 1, ej + 1, c, k], put)
 
     def finish_coarse(dst, i, values, curls):
         scaled = ckf[i]
@@ -270,6 +305,10 @@
         return jnp.where(column + b >= 4, jnp.int32(1), jnp.int32(0))
 
     def power(m):
+        if m > 8:
+            target = (lax.rem(n + m, slices), gx, gy)
+            copy = remote(ps.at[m - 1], arrived.at[m - 1], p_send.at[m - 1], p_recv.at[m - 1], target)
+            return copy, n + m < slices, n - m >= 0
         planes = m // 4 + carried(m % 4)
         copy = remote(ps.at[m - 1], arrived.at[m - 1], p_send.at[m - 1], p_recv.at[m - 1], along(planes, 0))
         sent = (planes > 0) & (plane + planes < 4)
@@ -277,9 +316,8 @@
         return copy, sent, received
 
     def one(src, dst, local, m):
-        sweep(src, dst, local, 24 - local, 63, finish_coarse)
-        for c in range(3):
-            ps[m - 1, c] = jnp.where(left_half, dst[c, 8:12, 0:8], pltpu.roll(dst[c, 12:16, 0:8], 64, 2))
+        folded_sweep(src, dst, local, finish_coarse)
+        ps[m - 1] = dst[:, 8:12, 0:8]
 
         copy, sent, _ = power(m)
         pl.when(sent)(copy.start)
@@ -291,15 +329,15 @@
                 one(src, dst, step, first + step)
 
     a_arrive()
+    pl.semaphore_wait(linked.at[1], 1)
+    pl.semaphore_wait(linked.at[2], 1)
     unpack(exa)
     phase(0)
 
     @pl.when(n < slices - 9)
     def _():
         exb[1, 1] = ps[7]
-        exchange(exb, b_send, b_recv)()
-        unpack(exb)
-        phase(8)
+        b_start()
 
     def across(b):
         return remote(zs.at[b - 1], zarr.at[b - 1], z_send.at[b - 1], z_recv.at[b - 1], along(0, b))
@@ -315,7 +353,7 @@
         def _(b=b):
             zs[b - 1] = jnp.zeros(zs.shape[1:], F32)
 
-        for m in range(b, slices, 4):
+        for m in (b, b + 4):
             copy, _, received = power(m)
 
             @pl.when(received)
@@ -325,20 +363,26 @@
 
         pl.when(kept)(across(b).start)
 
+    @pl.when(n < slices - 9)
+    def _():
+        b_arrive()
+        unpack(exb)
+        phase(8)
+
     acc[...] = jnp.zeros_like(acc)
-    for m in (4, 8, 12):
-        copy, _, received = power(m)
-
-        @pl.when(received)
-        def _(copy=copy, m=m):
-            copy.wait_recv()
-            acc[...] += arrived[m - 1]
-
     for b in (1, 2, 3):
         @pl.when((column >= b) | (plane > 0))
         def _(b=b):
             across(b).wait_recv()
             acc[...] += zarr[b - 1]
+
+    for m in (4, 8, 9, 10, 11, 12, 13, 14, 15):
+        copy, _, received = power(m)
+
+        @pl.when(received)
+        def _(copy=copy, m=m):
+            copy.wait_recv()
+            acc[...] += arrived[m - 1]
 
     for m in range(1, slices):
         copy, sent, _ = power(m)
@@ -355,7 +399,7 @@
         for c in range(3):
             for k in range(4):
                 for a in range(2):
-                    i = 2 * (4 * half + k) + a
+                    i = 2 * (7 - k if half else k) + a
                     for b in range(2):
                         cells = pl.ds(b, 8, stride=2)
                         out[0, c, i, cells] = w[c, 4 + i, cells] + wide[c, k]
@@ -388,13 +432,13 @@
             vmem(16, 3, 4, 8, 128),
             vmem(3, 3, 4, 8, 128),
             vmem(3, 3, 4, 8, 128),
-            vmem(3, 24, 24, 128),
-            vmem(3, 24, 24, 128),
-            vmem(24, 24, 128),
+            vmem(3, 12, 24, 128),
+            vmem(3, 12, 24, 128),
+            vmem(12, 24, 128),
             vmem(3, 4, 8, 128),
             dma(3),
             dma(8), dma(8), dma(8), dma(8), dma(8), dma(8), dma(8), dma(8),
-            dma(1), dma(1), dma(16), dma(16), dma(3), dma(3), pltpu.SemaphoreType.REGULAR,
+            dma(1), dma(1), dma(16), dma(16), dma(3), dma(3), pltpu.SemaphoreType.REGULAR((3,)),
         ],
         compiler_params=pltpu.CompilerParams(
             collective_id=0, has_side_effects=True, vmem_limit_bytes=60 * 1024 * 1024

time: 49.5 us -> 43.6 us (0.88)
  the two profiles are of different devices: /device:TPU:24 before, /device:TPU:1 now
where the time goes in v3:
time: 43.6 us; the launch traced here: 43.4 us
  Pallas kernels  41.7 us (96%)
  local copies, waits for them, and re-layouts  1.77 us (4%)
    pallas_call x1, Pallas kernels, body(): pl.pallas_call(kernel, out_shape=jax.ShapeDtypeStruct(state.shape, F32),...  41.7 us
    unnamed x1, local copies, waits for them, and re-layouts  1.77 us

profile of v3, /device:TPU:1, one launch (start us, length us, event | category | flops | bytes accessed | tf_op | source)
XLA Modules:
  0.0 43.4 jit_solution(18503705692021300)
XLA Ops:
  0.0 41.7 %parareal.1 = f32[1,3,16,16,128]{4,3,2,1,0:T(8,128)} custom-call(f32[1,3,16,16,128]{4,3,2,1,0:T(8,128)} %state.1, f32[1,4]{1,0:T(1,128)} %wave.1, f32[16]{0:T(128)} %cond.1, s32[16,16,128]{2,1,0:T(8,128)} %layer.1, s32[16,16,128]{2,1,0:T(8,128)} %mask.1), custom_call_target="tpu_custom_call" | custom-call | tf_op jit(solution)/shard_map/parareal/pallas_call | solution.py:413
  41.7 1.8 %copy.7 = f32[1,3,16,16,128]{4,3,2,1,0:T(8,128)} copy(f32[1,3,16,16,128]{4,3,2,1,0:T(8,128)} %parareal.1) | data formatting | bytes 786432

commit v4 on v3

--- a/solution.py
+++ b/solution.py
@@ -116,7 +116,7 @@
     state, wave, cond, layer, mask, out,
     w, v, near, far, lay, msk, sums, ck, exa, exb, rs, rs_next, ps, arrived, zs, zarr, c0, c1, ckf, acc,
     in_sem, fine_send, fine_recv, ck_send, ck_recv, a_send, a_recv, b_send, b_recv, rs_send, rs_recv, p_send, p_recv,
-    z_send, z_recv, linked,
+    z_send, z_recv, answers, whole,
 ):
     n, gx, gy = lax.axis_index("tm"), lax.axis_index("gx"), lax.axis_index("gy")
     slices = 16
@@ -136,6 +136,23 @@
         return pltpu.make_async_remote_copy(
             src_ref=src, dst_ref=dst, send_sem=ssem, recv_sem=rsem, device_id=device, device_id_type=MESH
         )
+
+    barrier = pltpu.get_barrier_semaphore()
+    for step in (1, 2, 3):
+
+        @pl.when(column + step < 4)
+        def _(step=step):
+            pl.semaphore_signal(barrier, inc=1, device_id=along(0, step), device_id_type=MESH)
+
+        @pl.when(plane + step < 4)
+        def _(step=step):
+            pl.semaphore_signal(barrier, inc=1, device_id=along(step, 0), device_id_type=MESH)
+
+    for di, dj in DIRS:
+
+        @pl.when(exists(di, dj))
+        def _(di=di, dj=dj):
+            pl.semaphore_signal(barrier, inc=1, device_id=beside(di, dj), device_id_type=MESH)
 
     loads = [
         pltpu.make_async_copy(state.at[0], w.at[0:3, 4:20, 0:16], in_sem.at[0]),
@@ -144,16 +161,6 @@
     ]
     for load in loads:
         load.start()
-
-    barrier = pltpu.get_barrier_semaphore()
-    for di, dj in DIRS:
-
-        @pl.when(exists(di, dj))
-        def _(di=di, dj=dj):
-            pl.semaphore_signal(barrier, inc=1, device_id=beside(di, dj), device_id_type=MESH)
-
-    for planes, columns in ((1, 0), (2, 0), (3, 0), (0, 1), (0, 3)):
-        pl.semaphore_signal(barrier, inc=1, device_id=along(planes, columns), device_id_type=MESH)
 
     @pl.when(gx == 0)
     def _():
@@ -193,9 +200,7 @@
     two, three = jnp.int32(2), jnp.int32(3)
     in_x = jnp.where((gx == 0) | (gx == 3), two, three)
     in_y = jnp.where((gy == 0) | (gy == 3), two, three)
-    pl.semaphore_wait(barrier, in_x * in_y - 1 + 5)
-    pl.semaphore_signal(linked.at[0], inc=1, device_id=along(0, 1), device_id_type=MESH)
-    pl.semaphore_signal(linked.at[1], inc=1, device_id=along(0, 3), device_id_type=MESH)
+    pl.semaphore_wait(barrier, in_x * in_y - 1 + plane + column)
 
     def fine_ends(di, dj):
         if dj == 0:
@@ -230,14 +235,22 @@
 
     fine_start, fine_arrive = swap(fine_ends, fine_send, fine_recv)
     fine_start()
+    for step in (1, 2, 3):
+
+        @pl.when(column - step >= 0)
+        def _(step=step):
+            pl.semaphore_signal(answers.at[step - 1], inc=1, device_id=along(0, -step), device_id_type=MESH)
+
+        @pl.when(plane - step >= 0)
+        def _(step=step):
+            pl.semaphore_signal(answers.at[3], inc=1, device_id=along(-step, 0), device_id_type=MESH)
+
     ck[1, 1] = restrict(lambda c, i, b: w[3, 4 + i, pl.ds(b, 8, stride=2)], 1, sums)[0]
     ck_start, ck_arrive = exchange(ck, ck_send, ck_recv)
     ck_start()
     rs[...] = restrict(lambda c, i, b: w[c, 4 + i, pl.ds(b, 8, stride=2)], 3, sums)
     rs_copy = remote(rs, rs_next, rs_send.at[0], rs_recv.at[0], (lax.rem(n + slices - 1, slices), gx, gy))
-    pl.semaphore_wait(linked.at[0], 1)
-    pl.semaphore_signal(linked.at[2], inc=1, device_id=along(0, 1), device_id_type=MESH)
-    pl.when(n > 0)(rs_copy.start)
+    pl.when(column > 0)(rs_copy.start)
 
     fine_arrive()
     for c in range(5):
@@ -265,11 +278,28 @@
         sweep(src, dst, 1 + step, 23 - step, finish)
 
     end = restrict(lambda c, i, b: w[c, 4 + i, pl.ds(b, 8, stride=2)], 3, sums)
+    @pl.when(column == 0)
+    def _():
+        pl.semaphore_wait(answers.at[2], 1)
+
+    pl.when((column == 0) & (n > 0))(rs_copy.start)
     pl.when(n < slices - 1)(rs_copy.wait_recv)
     pl.when(n > 0)(rs_copy.wait_send)
     exa[1, 1] = end - rs_next[...]
     a_start, a_arrive = exchange(exa, a_send, a_recv)
     a_start()
+    for step in (1, 2):
+
+        @pl.when(column + step < 4)
+        def _(step=step):
+            pl.semaphore_wait(answers.at[step - 1], 1)
+
+    @pl.when(plane < 3)
+    def _():
+        pl.semaphore_wait(answers.at[3], 3 - plane)
+
+    for step in (1, 2, 3):
+        pl.semaphore_signal(whole, inc=1, device_id=along(0, step), device_id_type=MESH)
     b_start, b_arrive = exchange(exb, b_send, b_recv)
 
     left_half = lax.broadcasted_iota(jnp.int32, (8, 128), 1) < 64
@@ -329,8 +359,6 @@
                 one(src, dst, step, first + step)
 
     a_arrive()
-    pl.semaphore_wait(linked.at[1], 1)
-    pl.semaphore_wait(linked.at[2], 1)
     unpack(exa)
     phase(0)
 
@@ -362,6 +390,8 @@
                 zs[b - 1] += arrived[m - 1]
 
         pl.when(kept)(across(b).start)
+
+    pl.semaphore_wait(whole, 3)
 
     @pl.when(n < slices - 9)
     def _():
@@ -438,7 +468,7 @@
             vmem(3, 4, 8, 128),
             dma(3),
             dma(8), dma(8), dma(8), dma(8), dma(8), dma(8), dma(8), dma(8),
-            dma(1), dma(1), dma(16), dma(16), dma(3), dma(3), pltpu.SemaphoreType.REGULAR((3,)),
+            dma(1), dma(1), dma(16), dma(16), dma(3), dma(3), pltpu.SemaphoreType.REGULAR((4,)), pltpu.SemaphoreType.REGULAR,
         ],
         compiler_params=pltpu.CompilerParams(
             collective_id=0, has_side_effects=True, vmem_limit_bytes=60 * 1024 * 1024

time: 43.6 us -> 42.1 us (0.966)
  the two profiles are of different devices: /device:TPU:1 before, /device:TPU:16 now
where the time goes in v4:
time: 42.1 us; the launch traced here: 42 us
  Pallas kernels  40.2 us (95%)
  local copies, waits for them, and re-layouts  1.77 us (4%)
    pallas_call x1, Pallas kernels, body(): pl.pallas_call(kernel, out_shape=jax.ShapeDtypeStruct(state.shape, F32),...  40.2 us
    unnamed x1, local copies, waits for them, and re-layouts  1.77 us

profile of v4, /device:TPU:16, one launch (start us, length us, event | category | flops | bytes accessed | tf_op | source)
XLA Modules:
  0.0 42.0 jit_solution(6018763541700426564)
XLA Ops:
  0.0 40.2 %parareal.1 = f32[1,3,16,16,128]{4,3,2,1,0:T(8,128)} custom-call(f32[1,3,16,16,128]{4,3,2,1,0:T(8,128)} %state.1, f32[1,4]{1,0:T(1,128)} %wave.1, f32[16]{0:T(128)} %cond.1, s32[16,16,128]{2,1,0:T(8,128)} %layer.1, s32[16,16,128]{2,1,0:T(8,128)} %mask.1), custom_call_target="tpu_custom_call" | custom-call | tf_op jit(solution)/shard_map/parareal/pallas_call | solution.py:443
  40.2 1.8 %copy.7 = f32[1,3,16,16,128]{4,3,2,1,0:T(8,128)} copy(f32[1,3,16,16,128]{4,3,2,1,0:T(8,128)} %parareal.1) | data formatting | bytes 786432

commit v5 on v4

--- a/solution.py
+++ b/solution.py
@@ -7,6 +7,7 @@
 
 DT = 0.015
 GROUP = 8
+DIRECT = (9, 10, 11, 12, 13, 14, 15)
 MESH = pl.DeviceIdType.MESH
 HIGHEST = lax.Precision.HIGHEST
 DIRS = [(-1, 0), (1, 0), (-1, -1), (1, 1), (-1, 1), (1, -1), (0, -1), (0, 1)]
@@ -114,8 +115,8 @@
 
 def kernel(
     state, wave, cond, layer, mask, out,
-    w, v, near, far, lay, msk, sums, ck, exa, exb, rs, rs_next, ps, arrived, zs, zarr, c0, c1, ckf, acc,
-    in_sem, fine_send, fine_recv, ck_send, ck_recv, a_send, a_recv, b_send, b_recv, rs_send, rs_recv, p_send, p_recv,
+    w, v, near, far, lay, msk, sums, ck, exs, exa, exb, ps, arrived, zs, zarr, c0, c1, lead, ckf, acc, held,
+    in_sem, fine_send, fine_recv, ck_send, ck_recv, a_send, a_recv, b_send, b_recv, s_send, s_recv, p_send, p_recv,
     z_send, z_recv, answers, whole,
 ):
     n, gx, gy = lax.axis_index("tm"), lax.axis_index("gx"), lax.axis_index("gy")
@@ -164,23 +165,23 @@
 
     @pl.when(gx == 0)
     def _():
-        for buf in (ck, exa, exb):
+        for buf in (ck, exs, exa, exb):
             buf[0] = jnp.zeros(buf.shape[1:], F32)
 
     @pl.when(gx == 3)
     def _():
-        for buf in (ck, exa, exb):
+        for buf in (ck, exs, exa, exb):
             buf[2] = jnp.zeros(buf.shape[1:], F32)
 
     @pl.when(gy == 0)
     def _():
-        for buf in (ck, exa, exb):
+        for buf in (ck, exs, exa, exb):
             buf[:, 0] = jnp.zeros((3,) + buf.shape[2:], F32)
         far[1] = jnp.zeros(far.shape[1:], F32)
 
     @pl.when(gy == 3)
     def _():
-        for buf in (ck, exa, exb):
+        for buf in (ck, exs, exa, exb):
             buf[:, 2] = jnp.zeros((3,) + buf.shape[2:], F32)
         far[0] = jnp.zeros(far.shape[1:], F32)
 
@@ -248,9 +249,9 @@
     ck[1, 1] = restrict(lambda c, i, b: w[3, 4 + i, pl.ds(b, 8, stride=2)], 1, sums)[0]
     ck_start, ck_arrive = exchange(ck, ck_send, ck_recv)
     ck_start()
-    rs[...] = restrict(lambda c, i, b: w[c, 4 + i, pl.ds(b, 8, stride=2)], 3, sums)
-    rs_copy = remote(rs, rs_next, rs_send.at[0], rs_recv.at[0], (lax.rem(n + slices - 1, slices), gx, gy))
-    pl.when(column > 0)(rs_copy.start)
+    exs[1, 1] = restrict(lambda c, i, b: w[c, 4 + i, pl.ds(b, 8, stride=2)], 3, sums)
+    s_start, s_arrive = exchange(exs, s_send, s_recv)
+    s_start()
 
     fine_arrive()
     for c in range(5):
@@ -278,17 +279,10 @@
         sweep(src, dst, 1 + step, 23 - step, finish)
 
     end = restrict(lambda c, i, b: w[c, 4 + i, pl.ds(b, 8, stride=2)], 3, sums)
-    @pl.when(column == 0)
-    def _():
-        pl.semaphore_wait(answers.at[2], 1)
-
-    pl.when((column == 0) & (n > 0))(rs_copy.start)
-    pl.when(n < slices - 1)(rs_copy.wait_recv)
-    pl.when(n > 0)(rs_copy.wait_send)
-    exa[1, 1] = end - rs_next[...]
+    exa[1, 1] = end
     a_start, a_arrive = exchange(exa, a_send, a_recv)
     a_start()
-    for step in (1, 2):
+    for step in (1, 2, 3):
 
         @pl.when(column + step < 4)
         def _(step=step):
@@ -318,11 +312,12 @@
 
     fold(lambda ei, ej, k: ck[ei + 1, ej + 1, k], put_kappa)
 
-    def unpack(buf):
+    def unpack(buf, less=None):
         for c in range(3):
 
             def put(row, tile, block, c=c):
-                c0[c, row, 8 * tile : 8 * tile + 8] = block
+                columns = slice(8 * tile, 8 * tile + 8)
+                c0[c, row, columns] = block if less is None else block - less[c, row, columns]
 
             fold(lambda ei, ej, k, c=c: buf[ei + 1, ej + 1, c, k], put)
 
@@ -335,7 +330,7 @@
         return jnp.where(column + b >= 4, jnp.int32(1), jnp.int32(0))
 
     def power(m):
-        if m > 8:
+        if m in DIRECT:
             target = (lax.rem(n + m, slices), gx, gy)
             copy = remote(ps.at[m - 1], arrived.at[m - 1], p_send.at[m - 1], p_recv.at[m - 1], target)
             return copy, n + m < slices, n - m >= 0
@@ -345,68 +340,84 @@
         received = (planes > 0) & (plane - planes >= 0)
         return copy, sent, received
 
-    def one(src, dst, local, m):
-        folded_sweep(src, dst, local, finish_coarse)
-        ps[m - 1] = dst[:, 8:12, 0:8]
-
-        copy, sent, _ = power(m)
-        pl.when(sent)(copy.start)
-
-    def phase(first):
-        for step in range(1, 9):
-            if first + step < slices:
-                src, dst = (c0, c1) if step % 2 else (c1, c0)
-                one(src, dst, step, first + step)
+    def one(src, dst, low, m):
+        @pl.when(n + m < slices)
+        def _():
+            folded_sweep(src, dst, low, finish_coarse)
+            ps[m - 1] = dst[:, 8:12, 0:8]
+            copy, sent, _ = power(m)
+            pl.when(sent)(copy.start)
+
+    s_arrive()
+    unpack(exs)
+    folded_sweep(c0, lead, 1, finish_coarse)
+
+    @pl.when(n == 0)
+    def _():
+        lead[...] = jnp.zeros_like(lead)
 
     a_arrive()
-    unpack(exa)
-    phase(0)
-
-    @pl.when(n < slices - 9)
-    def _():
-        exb[1, 1] = ps[7]
+    pl.semaphore_wait(whole, 3)
+    unpack(exa, lead)
+    for m in range(1, 8):
+        src, dst = (c0, c1) if m % 2 else (c1, c0)
+        one(src, dst, m + 1, m)
+
+    @pl.when(n < slices - 8)
+    def _():
+        exb[1, 1] = ps[6]
         b_start()
 
     def across(b):
         return remote(zs.at[b - 1], zarr.at[b - 1], z_send.at[b - 1], z_recv.at[b - 1], along(0, b))
 
     for b in (1, 2, 3):
-        kept = plane >= carried(b)
-
-        @pl.when(carried(b) == 0)
-        def _(b=b):
-            zs[b - 1] = ps[b - 1]
-
-        @pl.when(carried(b) == 1)
-        def _(b=b):
-            zs[b - 1] = jnp.zeros(zs.shape[1:], F32)
-
         for m in (b, b + 4):
+            if m in DIRECT:
+                continue
             copy, _, received = power(m)
+            first = m == b or b in DIRECT
+
+            if m == b:
+
+                @pl.when(carried(b) == 0)
+                def _(b=b):
+                    zs[b - 1] = ps[b - 1]
 
             @pl.when(received)
-            def _(copy=copy, m=m, b=b):
+            def _(copy=copy, m=m, b=b, first=first):
                 copy.wait_recv()
-                zs[b - 1] += arrived[m - 1]
-
-        pl.when(kept)(across(b).start)
-
-    pl.semaphore_wait(whole, 3)
-
-    @pl.when(n < slices - 9)
+                if first:
+                    zs[b - 1] = arrived[m - 1]
+                else:
+                    zs[b - 1] += arrived[m - 1]
+
+        if b not in DIRECT:
+            pl.when(plane >= carried(b))(across(b).start)
+        elif b + 4 not in DIRECT:
+            pl.when(plane >= 1 + carried(b))(across(b).start)
+
+    @pl.when(n < slices - 8)
     def _():
         b_arrive()
         unpack(exb)
-        phase(8)
-
-    acc[...] = jnp.zeros_like(acc)
+        for m in range(8, slices):
+            src, dst = (c1, c0) if m % 2 else (c0, c1)
+            one(src, dst, m - 7, m)
+
+    acc[...] = -lead[:, 8:12, 0:8]
     for b in (1, 2, 3):
-        @pl.when((column >= b) | (plane > 0))
+        if b in DIRECT and b + 4 in DIRECT:
+            continue
+
+        late = 1 if b in DIRECT else 0
+
+        @pl.when(plane >= late + jnp.where(column >= b, jnp.int32(0), jnp.int32(1)))
         def _(b=b):
             across(b).wait_recv()
             acc[...] += zarr[b - 1]
 
-    for m in (4, 8, 9, 10, 11, 12, 13, 14, 15):
+    for m in sorted({4, 8, 12, *DIRECT}):
         copy, _, received = power(m)
 
         @pl.when(received)
@@ -414,25 +425,35 @@
             copy.wait_recv()
             acc[...] += arrived[m - 1]
 
-    for m in range(1, slices):
-        copy, sent, _ = power(m)
-        pl.when(sent)(copy.wait_send)
-    for b in (1, 2, 3):
-        pl.when(plane >= carried(b))(across(b).wait_send)
-
     z = lax.broadcasted_iota(jnp.int32, (128, 128), 1)
     lane = lax.broadcasted_iota(jnp.int32, (128, 128), 0)
     packed = acc[...].reshape(96, 128)
+    wide = []
     for half in range(2):
         pick = jnp.where(lane == z // 2 + 64 * half, 1.0, 0.0).astype(F32)
-        wide = jnp.dot(packed, pick, precision=HIGHEST, preferred_element_type=F32).reshape(3, 4, 8, 128)
-        for c in range(3):
+        wide.append(jnp.dot(packed, pick, precision=HIGHEST, preferred_element_type=F32).reshape(3, 4, 8, 128))
+    stores = []
+    for c in range(3):
+        for half in range(2):
             for k in range(4):
                 for a in range(2):
                     i = 2 * (7 - k if half else k) + a
                     for b in range(2):
                         cells = pl.ds(b, 8, stride=2)
-                        out[0, c, i, cells] = w[c, 4 + i, cells] + wide[c, k]
+                        held[c, i, cells] = w[c, 4 + i, cells] + wide[half][c, k]
+        stores.append(pltpu.make_async_copy(held.at[c], out.at[0, c], in_sem.at[c]))
+        stores[c].start()
+
+    for m in range(1, slices):
+        copy, sent, _ = power(m)
+        pl.when(sent)(copy.wait_send)
+    for b in (1, 2, 3):
+        if b not in DIRECT:
+            pl.when(plane >= carried(b))(across(b).wait_send)
+        elif b + 4 not in DIRECT:
+            pl.when(plane >= 1 + carried(b))(across(b).wait_send)
+    for store in stores:
+        store.wait()
 
 
 def body(state, waveform, conductivity, layer_map, loop_mask):
@@ -444,7 +465,7 @@
         kernel,
         out_shape=jax.ShapeDtypeStruct(state.shape, F32),
         in_specs=[any_space, smem, smem, any_space, any_space],
-        out_specs=pl.BlockSpec(memory_space=pltpu.VMEM),
+        out_specs=any_space,
         scratch_shapes=[
             vmem(5, 24, 24, 128),
             vmem(3, 24, 24, 128),
@@ -456,19 +477,20 @@
             vmem(3, 3, 4, 8, 128),
             vmem(3, 3, 3, 4, 8, 128),
             vmem(3, 3, 3, 4, 8, 128),
-            vmem(3, 4, 8, 128),
-            vmem(3, 4, 8, 128),
+            vmem(3, 3, 3, 4, 8, 128),
             vmem(16, 3, 4, 8, 128),
             vmem(16, 3, 4, 8, 128),
             vmem(3, 3, 4, 8, 128),
             vmem(3, 3, 4, 8, 128),
             vmem(3, 12, 24, 128),
             vmem(3, 12, 24, 128),
+            vmem(3, 12, 24, 128),
             vmem(12, 24, 128),
             vmem(3, 4, 8, 128),
+            vmem(3, 16, 16, 128),
             dma(3),
             dma(8), dma(8), dma(8), dma(8), dma(8), dma(8), dma(8), dma(8),
-            dma(1), dma(1), dma(16), dma(16), dma(3), dma(3), pltpu.SemaphoreType.REGULAR((4,)), pltpu.SemaphoreType.REGULAR,
+            dma(8), dma(8), dma(16), dma(16), dma(3), dma(3), pltpu.SemaphoreType.REGULAR((4,)), pltpu.SemaphoreType.REGULAR,
         ],
         compiler_params=pltpu.CompilerParams(
             collective_id=0, has_side_effects=True, vmem_limit_bytes=60 * 1024 * 1024

time: 42.1 us -> 41.5 us (0.986)
  the two profiles are of different devices: /device:TPU:16 before, /device:TPU:24 now
where the time goes in v5:
time: 41.5 us; the launch traced here: 41.2 us
  Pallas kernels  39.4 us (95%)
  local copies, waits for them, and re-layouts  1.77 us (4%)
    pallas_call x1, Pallas kernels, body(): pl.pallas_call(kernel, out_shape=jax.ShapeDtypeStruct(state.shape, F32),...  39.4 us
    unnamed x1, local copies, waits for them, and re-layouts  1.77 us

profile of v5, /device:TPU:24, one launch (start us, length us, event | category | flops | bytes accessed | tf_op | source)
XLA Modules:
  0.0 41.2 jit_solution(11476169565607131140)
XLA Ops:
  0.0 39.4 %parareal.1 = f32[1,3,16,16,128]{4,3,2,1,0:T(8,128)} custom-call(f32[1,3,16,16,128]{4,3,2,1,0:T(8,128)} %state.1, f32[1,4]{1,0:T(1,128)} %wave.1, f32[16]{0:T(128)} %cond.1, s32[16,16,128]{2,1,0:T(8,128)} %layer.1, s32[16,16,128]{2,1,0:T(8,128)} %mask.1), custom_call_target="tpu_custom_call" | custom-call | tf_op jit(solution)/shard_map/parareal/pallas_call | solution.py:464
  39.4 1.8 %copy.7 = f32[1,3,16,16,128]{4,3,2,1,0:T(8,128)} copy(f32[1,3,16,16,128]{4,3,2,1,0:T(8,128)} %parareal.1) | data formatting | bytes 786432

commit v6 on v5

--- a/solution.py
+++ b/solution.py
@@ -7,7 +7,6 @@
 
 DT = 0.015
 GROUP = 8
-DIRECT = (9, 10, 11, 12, 13, 14, 15)
 MESH = pl.DeviceIdType.MESH
 HIGHEST = lax.Precision.HIGHEST
 DIRS = [(-1, 0), (1, 0), (-1, -1), (1, 1), (-1, 1), (1, -1), (0, -1), (0, 1)]
@@ -67,16 +66,19 @@
         carry = row(low + GROUP * groups + k, carry)
 
 
-def folded_sweep(src, dst, low, finish):
-    col_next, col_prev, z_next, z_prev = shifts(24, 64)
-    left = lax.broadcasted_iota(jnp.int32, (24, 128), 1) < 64
+def folded_sweep(src, dst, low, width, finish):
+    col_next, col_prev, z_next, z_prev = shifts(width, 64)
+    left = lax.broadcasted_iota(jnp.int32, (width, 128), 1) < 64
+
+    def load(c, p):
+        return src[c, p, 0:width]
 
     def row_next(c, p, x):
-        after = src[c, p + 1] if p < 11 else pltpu.roll(x, 64, 1)
-        return jnp.where(left, after, src[c, p - 1] if p >= low else x)
+        after = load(c, p + 1) if p < 11 else pltpu.roll(x, 64, 1)
+        return jnp.where(left, after, load(c, p - 1) if p >= low else x)
 
     def twists(p):
-        v0, v1, v2 = src[0, p], src[1, p], src[2, p]
+        v0, v1, v2 = load(0, p), load(1, p), load(2, p)
         h1 = (z_next(v0) - v0) - (row_next(2, p, v2) - v2)
         h2 = (row_next(1, p, v1) - v1) - (col_next(v0) - v0)
         return (v0, v1, v2), h1, h2
@@ -115,9 +117,9 @@
 
 def kernel(
     state, wave, cond, layer, mask, out,
-    w, v, near, far, lay, msk, sums, ck, exs, exa, exb, ps, arrived, zs, zarr, c0, c1, lead, ckf, acc, held,
+    w, v, near, far, lay, msk, sums, ck, exs, exa, exb, ps, arrived, straight, zs, zarr, c0, c1, lead, ckf, ckn, acc, held,
     in_sem, fine_send, fine_recv, ck_send, ck_recv, a_send, a_recv, b_send, b_recv, s_send, s_recv, p_send, p_recv,
-    z_send, z_recv, answers, whole,
+    z_send, z_recv, d_recv, answers, whole,
 ):
     n, gx, gy = lax.axis_index("tm"), lax.axis_index("gx"), lax.axis_index("gy")
     slices = 16
@@ -326,38 +328,68 @@
         for c in range(3):
             dst[c, i] = values[c] - scaled * curls[c]
 
+    right_side = lax.broadcasted_iota(jnp.int32, (8, 128), 0) < 4
+
+    def finish_narrow(dst, i, values, curls):
+        scaled = ckn[i]
+        for c in range(3):
+            dst[c, i, 0:16] = values[c] - scaled * curls[c]
+
+    def narrow(buf):
+        for c in range(3):
+            for p in range(4, 12):
+                buf[c, p, 8:16] = jnp.where(right_side, buf[c, p, 8:16], buf[c, p, 16:24])
+
+    for p in range(4, 12):
+        ckn[p, 0:8] = ckf[p, 0:8]
+        ckn[p, 8:16] = jnp.where(right_side, ckf[p, 8:16], ckf[p, 16:24])
+
     def carried(b):
         return jnp.where(column + b >= 4, jnp.int32(1), jnp.int32(0))
 
     def power(m):
-        if m in DIRECT:
-            target = (lax.rem(n + m, slices), gx, gy)
-            copy = remote(ps.at[m - 1], arrived.at[m - 1], p_send.at[m - 1], p_recv.at[m - 1], target)
-            return copy, n + m < slices, n - m >= 0
-        planes = m // 4 + carried(m % 4)
-        copy = remote(ps.at[m - 1], arrived.at[m - 1], p_send.at[m - 1], p_recv.at[m - 1], along(planes, 0))
-        sent = (planes > 0) & (plane + planes < 4)
-        received = (planes > 0) & (plane - planes >= 0)
-        return copy, sent, received
+        over = carried(m % 4)
+
+        def to(buf, sem, target):
+            return remote(ps.at[m - 1], buf, p_send.at[m - 1], sem, target)
+
+        ahead = (lax.rem(n + m, slices), gx, gy)
+        if m > 11:
+            return [(to(arrived.at[m - 1], p_recv.at[m - 1], ahead), n + m < slices, n - m >= 0)]
+        planes = m // 4 + over
+        along_y = to(arrived.at[m - 1], p_recv.at[m - 1], along(planes, 0))
+        if m < 9:
+            return [(along_y, (planes > 0) & (plane + planes < 4), (planes > 0) & (plane - planes >= 0))]
+        b = m - 8
+        direct = to(straight.at[b - 1], d_recv.at[b - 1], ahead)
+        return [
+            (along_y, (over == 0) & (plane < 2), (over == 0) & (plane >= 2)),
+            (direct, (over == 1) & (n + m < slices), (column < b) & (n - m >= 0)),
+        ]
 
     def one(src, dst, low, m):
         @pl.when(n + m < slices)
         def _():
-            folded_sweep(src, dst, low, finish_coarse)
+            if low == 5:
+                narrow(src)
+            if low < 5:
+                folded_sweep(src, dst, low, 24, finish_coarse)
+            else:
+                folded_sweep(src, dst, low, 16, finish_narrow)
             ps[m - 1] = dst[:, 8:12, 0:8]
-            copy, sent, _ = power(m)
-            pl.when(sent)(copy.start)
+            if m != 4:
+                for copy, sent, _ in power(m):
+                    pl.when(sent)(copy.start)
 
     s_arrive()
     unpack(exs)
-    folded_sweep(c0, lead, 1, finish_coarse)
+    folded_sweep(c0, lead, 1, 24, finish_coarse)
 
     @pl.when(n == 0)
     def _():
         lead[...] = jnp.zeros_like(lead)
 
     a_arrive()
-    pl.semaphore_wait(whole, 3)
     unpack(exa, lead)
     for m in range(1, 8):
         src, dst = (c0, c1) if m % 2 else (c1, c0)
@@ -368,34 +400,44 @@
         exb[1, 1] = ps[6]
         b_start()
 
+    copy, sent, _ = power(4)[0]
+    pl.when(sent)(copy.start)
+
     def across(b):
         return remote(zs.at[b - 1], zarr.at[b - 1], z_send.at[b - 1], z_recv.at[b - 1], along(0, b))
 
-    for b in (1, 2, 3):
-        for m in (b, b + 4):
-            if m in DIRECT:
-                continue
-            copy, _, received = power(m)
-            first = m == b or b in DIRECT
-
-            if m == b:
-
-                @pl.when(carried(b) == 0)
-                def _(b=b):
-                    zs[b - 1] = ps[b - 1]
+    def relay(b):
+        @pl.when(carried(b) == 0)
+        def _():
+            zs[b - 1] = ps[b - 1]
+
+        @pl.when(carried(b) == 1)
+        def _():
+            zs[b - 1] = jnp.zeros(zs.shape[1:], F32)
+
+        for m in (b, b + 4, b + 8):
+            copy, _, received = power(m)[0]
 
             @pl.when(received)
-            def _(copy=copy, m=m, b=b, first=first):
+            def _(copy=copy, m=m):
                 copy.wait_recv()
-                if first:
-                    zs[b - 1] = arrived[m - 1]
-                else:
-                    zs[b - 1] += arrived[m - 1]
-
-        if b not in DIRECT:
-            pl.when(plane >= carried(b))(across(b).start)
-        elif b + 4 not in DIRECT:
-            pl.when(plane >= 1 + carried(b))(across(b).start)
+                zs[b - 1] += arrived[m - 1]
+
+        pl.when(plane >= carried(b))(across(b).start)
+
+    for b in (2, 1, 3):
+
+        @pl.when(carried(b) == 1)
+        def _(b=b):
+            relay(b)
+
+    for b in (2, 1, 3):
+
+        @pl.when(carried(b) == 0)
+        def _(b=b):
+            relay(b)
+
+    pl.semaphore_wait(whole, 3)
 
     @pl.when(n < slices - 8)
     def _():
@@ -406,24 +448,23 @@
             one(src, dst, m - 7, m)
 
     acc[...] = -lead[:, 8:12, 0:8]
+    def take(copy, received, block):
+        @pl.when(received)
+        def _():
+            copy.wait_recv()
+            acc[...] += block[...]
+
+    for m in (4, 8):
+        copy, _, received = power(m)[0]
+        take(copy, received, arrived.at[m - 1])
     for b in (1, 2, 3):
-        if b in DIRECT and b + 4 in DIRECT:
-            continue
-
-        late = 1 if b in DIRECT else 0
-
-        @pl.when(plane >= late + jnp.where(column >= b, jnp.int32(0), jnp.int32(1)))
-        def _(b=b):
-            across(b).wait_recv()
-            acc[...] += zarr[b - 1]
-
-    for m in sorted({4, 8, 12, *DIRECT}):
-        copy, _, received = power(m)
-
-        @pl.when(received)
-        def _(copy=copy, m=m):
-            copy.wait_recv()
-            acc[...] += arrived[m - 1]
+        take(across(b), (column >= b) | (plane > 0), zarr.at[b - 1])
+    for m in (9, 10, 11):
+        copy, _, received = power(m)[1]
+        take(copy, received, straight.at[m - 9])
+    for m in (12, 13, 14, 15):
+        copy, _, received = power(m)[0]
+        take(copy, received, arrived.at[m - 1])
 
     z = lax.broadcasted_iota(jnp.int32, (128, 128), 1)
     lane = lax.broadcasted_iota(jnp.int32, (128, 128), 0)
@@ -445,13 +486,10 @@
         stores[c].start()
 
     for m in range(1, slices):
-        copy, sent, _ = power(m)
-        pl.when(sent)(copy.wait_send)
+        for copy, sent, _ in power(m):
+            pl.when(sent)(copy.wait_send)
     for b in (1, 2, 3):
-        if b not in DIRECT:
-            pl.when(plane >= carried(b))(across(b).wait_send)
-        elif b + 4 not in DIRECT:
-            pl.when(plane >= 1 + carried(b))(across(b).wait_send)
+        pl.when(plane >= carried(b))(across(b).wait_send)
     for store in stores:
         store.wait()
 
@@ -482,15 +520,17 @@
             vmem(16, 3, 4, 8, 128),
             vmem(3, 3, 4, 8, 128),
             vmem(3, 3, 4, 8, 128),
+            vmem(3, 3, 4, 8, 128),
             vmem(3, 12, 24, 128),
             vmem(3, 12, 24, 128),
             vmem(3, 12, 24, 128),
             vmem(12, 24, 128),
+            vmem(12, 16, 128),
             vmem(3, 4, 8, 128),
             vmem(3, 16, 16, 128),
             dma(3),
             dma(8), dma(8), dma(8), dma(8), dma(8), dma(8), dma(8), dma(8),
-            dma(8), dma(8), dma(16), dma(16), dma(3), dma(3), pltpu.SemaphoreType.REGULAR((4,)), pltpu.SemaphoreType.REGULAR,
+            dma(8), dma(8), dma(16), dma(16), dma(3), dma(3), dma(3), pltpu.SemaphoreType.REGULAR((4,)), pltpu.SemaphoreType.REGULAR,
         ],
         compiler_params=pltpu.CompilerParams(
             collective_id=0, has_side_effects=True, vmem_limit_bytes=60 * 1024 * 1024

time: 41.5 us -> 40.1 us (0.966)
  Pallas kernels: 39.4 us -> 37.6 us
    pallas_call x1, Pallas kernels: 39.4 us -> 37.6 us  [body(): pl.pallas_call(kernel, out_shape=jax.ShapeDtypeStruct(state.shape, F32),...]
where the time goes in v6:
time: 40.1 us; the launch traced here: 39.4 us
  Pallas kernels  37.6 us (94%)
  local copies, waits for them, and re-layouts  1.77 us (4%)
    pallas_call x1, Pallas kernels, body(): pl.pallas_call(kernel, out_shape=jax.ShapeDtypeStruct(state.shape, F32),...  37.6 us
    unnamed x1, local copies, waits for them, and re-layouts  1.77 us

profile of v6, /device:TPU:24, one launch (start us, length us, event | category | flops | bytes accessed | tf_op | source)
XLA Modules:
  0.0 39.4 jit_solution(11934412766701970354)
XLA Ops:
  0.0 37.6 %parareal.1 = f32[1,3,16,16,128]{4,3,2,1,0:T(8,128)} custom-call(f32[1,3,16,16,128]{4,3,2,1,0:T(8,128)} %state.1, f32[1,4]{1,0:T(1,128)} %wave.1, f32[16]{0:T(128)} %cond.1, s32[16,16,128]{2,1,0:T(8,128)} %layer.1, s32[16,16,128]{2,1,0:T(8,128)} %mask.1), custom_call_target="tpu_custom_call" | custom-call | tf_op jit(solution)/shard_map/parareal/pallas_call | solution.py:502
  37.6 1.8 %copy.7 = f32[1,3,16,16,128]{4,3,2,1,0:T(8,128)} copy(f32[1,3,16,16,128]{4,3,2,1,0:T(8,128)} %parareal.1) | data formatting | bytes 786432

commit v7 on v6

--- a/solution.py
+++ b/solution.py
@@ -9,7 +9,7 @@
 GROUP = 8
 MESH = pl.DeviceIdType.MESH
 HIGHEST = lax.Precision.HIGHEST
-DIRS = [(-1, 0), (1, 0), (-1, -1), (1, 1), (-1, 1), (1, -1), (0, -1), (0, 1)]
+DIRS = [(-1, -1), (1, 1), (-1, 1), (1, -1), (-1, 0), (1, 0), (0, -1), (0, 1)]
 F32 = jnp.float32
 
 
@@ -253,9 +253,9 @@
     ck_start()
     exs[1, 1] = restrict(lambda c, i, b: w[c, 4 + i, pl.ds(b, 8, stride=2)], 3, sums)
     s_start, s_arrive = exchange(exs, s_send, s_recv)
+
+    fine_arrive()
     s_start()
-
-    fine_arrive()
     for c in range(5):
         w[c, :, 16:20] = far[0, c]
         w[c, :, 20:24] = far[1, c]

time: 40.1 us -> 38.9 us (0.970)
  Pallas kernels: 37.6 us -> 36.8 us
    pallas_call x1, Pallas kernels: 37.6 us -> 36.8 us  [body(): pl.pallas_call(kernel, out_shape=jax.ShapeDtypeStruct(state.shape, F32),...]
where the time goes in v7:
time: 38.9 us; the launch traced here: 38.5 us
  Pallas kernels  36.8 us (95%)
  local copies, waits for them, and re-layouts  1.77 us (5%)
    pallas_call x1, Pallas kernels, body(): pl.pallas_call(kernel, out_shape=jax.ShapeDtypeStruct(state.shape, F32),...  36.8 us
    unnamed x1, local copies, waits for them, and re-layouts  1.77 us

profile of v7, /device:TPU:24, one launch (start us, length us, event | category | flops | bytes accessed | tf_op | source)
XLA Modules:
  0.0 38.5 jit_solution(3392729111963401073)
XLA Ops:
  0.0 36.8 %parareal.1 = f32[1,3,16,16,128]{4,3,2,1,0:T(8,128)} custom-call(f32[1,3,16,16,128]{4,3,2,1,0:T(8,128)} %state.1, f32[1,4]{1,0:T(1,128)} %wave.1, f32[16]{0:T(128)} %cond.1, s32[16,16,128]{2,1,0:T(8,128)} %layer.1, s32[16,16,128]{2,1,0:T(8,128)} %mask.1), custom_call_target="tpu_custom_call" | custom-call | tf_op jit(solution)/shard_map/parareal/pallas_call | solution.py:502
  36.8 1.8 %copy.7 = f32[1,3,16,16,128]{4,3,2,1,0:T(8,128)} copy(f32[1,3,16,16,128]{4,3,2,1,0:T(8,128)} %parareal.1) | data formatting | bytes 786432

commit v8 on v7

--- a/solution.py
+++ b/solution.py
@@ -228,15 +228,17 @@
         def finish():
             for copy, di, dj in copies:
                 pl.when(exists(-di, -dj))(copy.wait_recv)
+
+        def sent():
             for copy, di, dj in copies:
                 pl.when(exists(di, dj))(copy.wait_send)
 
-        return start, finish
+        return start, finish, sent
 
     def exchange(buf, ssem, rsem):
         return swap(lambda di, dj: (buf.at[1, 1], buf.at[1 - di, 1 - dj]), ssem, rsem)
 
-    fine_start, fine_arrive = swap(fine_ends, fine_send, fine_recv)
+    fine_start, fine_arrive, fine_sent = swap(fine_ends, fine_send, fine_recv)
     fine_start()
     for step in (1, 2, 3):
 
@@ -249,10 +251,10 @@
             pl.semaphore_signal(answers.at[3], inc=1, device_id=along(-step, 0), device_id_type=MESH)
 
     ck[1, 1] = restrict(lambda c, i, b: w[3, 4 + i, pl.ds(b, 8, stride=2)], 1, sums)[0]
-    ck_start, ck_arrive = exchange(ck, ck_send, ck_recv)
+    ck_start, ck_arrive, ck_sent = exchange(ck, ck_send, ck_recv)
     ck_start()
     exs[1, 1] = restrict(lambda c, i, b: w[c, 4 + i, pl.ds(b, 8, stride=2)], 3, sums)
-    s_start, s_arrive = exchange(exs, s_send, s_recv)
+    s_start, s_arrive, s_sent = exchange(exs, s_send, s_recv)
 
     fine_arrive()
     s_start()
@@ -278,11 +280,13 @@
             dst[2, i] = values[2] - scaled * curls[2]
 
         src, dst = (w, v) if step % 2 == 0 else (v, w)
+        if step == 1:
+            fine_sent()
         sweep(src, dst, 1 + step, 23 - step, finish)
 
     end = restrict(lambda c, i, b: w[c, 4 + i, pl.ds(b, 8, stride=2)], 3, sums)
     exa[1, 1] = end
-    a_start, a_arrive = exchange(exa, a_send, a_recv)
+    a_start, a_arrive, a_sent = exchange(exa, a_send, a_recv)
     a_start()
     for step in (1, 2, 3):
 
@@ -296,7 +300,7 @@
 
     for step in (1, 2, 3):
         pl.semaphore_signal(whole, inc=1, device_id=along(0, step), device_id_type=MESH)
-    b_start, b_arrive = exchange(exb, b_send, b_recv)
+    b_start, b_arrive, b_sent = exchange(exb, b_send, b_recv)
 
     left_half = lax.broadcasted_iota(jnp.int32, (8, 128), 1) < 64
 
@@ -490,6 +494,10 @@
             pl.when(sent)(copy.wait_send)
     for b in (1, 2, 3):
         pl.when(plane >= carried(b))(across(b).wait_send)
+    ck_sent()
+    s_sent()
+    a_sent()
+    pl.when(n < slices - 8)(b_sent)
     for store in stores:
         store.wait()
 

time: 38.9 us -> 39 us (level)
  no operation moved by 1% of the time
where the time goes in v8:
time: 39 us; the launch traced here: 38.6 us
  Pallas kernels  36.8 us (94%)
  local copies, waits for them, and re-layouts  1.77 us (5%)
    pallas_call x1, Pallas kernels, body(): pl.pallas_call(kernel, out_shape=jax.ShapeDtypeStruct(state.shape, F32),...  36.8 us
    unnamed x1, local copies, waits for them, and re-layouts  1.77 us

profile of v8, /device:TPU:24, one launch (start us, length us, event | category | flops | bytes accessed | tf_op | source)
XLA Modules:
  0.0 38.6 jit_solution(14750501794920440205)
XLA Ops:
  0.0 36.8 %parareal.1 = f32[1,3,16,16,128]{4,3,2,1,0:T(8,128)} custom-call(f32[1,3,16,16,128]{4,3,2,1,0:T(8,128)} %state.1, f32[1,4]{1,0:T(1,128)} %wave.1, f32[16]{0:T(128)} %cond.1, s32[16,16,128]{2,1,0:T(8,128)} %layer.1, s32[16,16,128]{2,1,0:T(8,128)} %mask.1), custom_call_target="tpu_custom_call" | custom-call | tf_op jit(solution)/shard_map/parareal/pallas_call | solution.py:510
  36.9 1.8 %copy.7 = f32[1,3,16,16,128]{4,3,2,1,0:T(8,128)} copy(f32[1,3,16,16,128]{4,3,2,1,0:T(8,128)} %parareal.1) | data formatting | bytes 786432
